TPU v7x, 256 devices: a whole 4x4x8 slice. The times are simulated.
256 devices in a mesh: seq: 64 (over y, z, core), head: 4 (over x).
Axes of the slice: x: 4, y: 4, z: 8, core: 2. Of those that a mesh axis runs over, the one named last changes fastest.
Arguments:
- queries: bfloat16 [196608, 1024], P('seq', 'head'), may hold values from -5 to 5
- keys: bfloat16 [196608, 128], P('seq'), may hold values from -5 to 5
- values: bfloat16 [196608, 128], P('seq'), may hold values from -6 to 6
- selected: int32 [384, 3], P('seq'), may hold values from 0 to 382, as said below
Outputs:
- attended: bfloat16 [196608, 1024], P('seq', 'head')
Inputs may be any that keep to these rules, and one draw needn't show every extreme that they name: Every nonzero selected[b, j] is a block before b. The selections of the 6 query blocks held by one index of seq name at most one block of each other index. A 0 marks an empty slot.
All inputs are finite; a program needn't handle non-finite values.
Results may differ from a plain program's by a relative error of at most 0.0049.
Values may be sent and summed in bfloat16 or wider, within the bound.
A program may use at most 128 MiB of HBM per device.

v0:
```python
import math

import jax
import jax.numpy as jnp
from jax import lax
from jax.sharding import PartitionSpec as P


def from_root(value, axis, source):
    kept = jnp.where(lax.axis_index(axis) == source, value, 0).astype(value.dtype)
    return lax.psum(kept, axis)


def live_slots(chosen):
    nonzero = chosen != 0
    equal = chosen[:, :, None] == chosen[:, None, :]
    order = jnp.arange(chosen.shape[1])
    earlier = order[None, :] < order[:, None]
    repeated = jnp.any(equal & earlier[None, :, :], axis=2)
    return nonzero & jnp.logical_not(repeated)


def shards(queries, keys, values, selected):
    seq_count = lax.axis_size("seq")
    my_index = lax.axis_index("seq")
    blocks_here, per_block = selected.shape
    head_size = keys.shape[1]
    block_len = keys.shape[0] // blocks_here
    heads_here = queries.shape[1] // head_size
    key_blocks = keys.reshape(blocks_here, block_len, head_size)
    value_blocks = values.reshape(blocks_here, block_len, head_size)
    owner = (selected // blocks_here).reshape(-1)
    local_index = (selected % blocks_here).reshape(-1)
    remote = owner != my_index
    owner_list = jnp.arange(seq_count, dtype=jnp.int32)
    hits = (owner[:, None] == owner_list[None, :]) & remote[:, None]
    wanted = jnp.sum(jnp.where(hits, local_index[:, None], 0), axis=0)
    asked = lax.all_to_all(
        wanted.reshape(seq_count, 1), "seq", split_axis=0, concat_axis=0, tiled=True
    ).reshape(seq_count)
    zero_keys, zero_values = (
        from_root(key_blocks[0], "seq", 0),
        from_root(value_blocks[0], "seq", 0),
    )
    got_keys, got_values = (
        lax.all_to_all(key_blocks[asked], "seq", split_axis=0, concat_axis=0, tiled=True),
        lax.all_to_all(value_blocks[asked], "seq", split_axis=0, concat_axis=0, tiled=True),
    )
    fetched_keys = got_keys[owner]
    fetched_values = got_values[owner]
    slot_keys = jnp.where(remote[:, None, None], fetched_keys, key_blocks[local_index])
    slot_values = jnp.where(remote[:, None, None], fetched_values, value_blocks[local_index])
    slot_keys = slot_keys.reshape(blocks_here, per_block, block_len, head_size)
    slot_values = slot_values.reshape(blocks_here, per_block, block_len, head_size)
    live = live_slots(selected)
    numbers = my_index * blocks_here + jnp.arange(blocks_here, dtype=jnp.int32)
    query_blocks = queries.reshape(blocks_here, block_len, heads_here, head_size)
    scale = 1.0 / math.sqrt(head_size)
    position = jnp.arange(block_len)
    causal = position[None, :] <= position[:, None]

    def attend_block(inputs):
        query_here, own_keys, own_values, picked_keys, picked_values, live_here, number = inputs
        tiles_k = jnp.concatenate([zero_keys[None], own_keys[None], picked_keys], axis=0)
        tiles_v = jnp.concatenate([zero_values[None], own_values[None], picked_values], axis=0)
        tiles_k = tiles_k.reshape((per_block + 2) * block_len, head_size)
        tiles_v = tiles_v.reshape((per_block + 2) * block_len, head_size)
        tile_live = jnp.concatenate(
            [jnp.reshape(number != 0, (1,)), jnp.ones((1,), bool), live_here]
        )
        allowed = jnp.broadcast_to(tile_live[None, :, None], (block_len, per_block + 2, block_len))
        allowed = allowed.at[:, 1, :].set(causal)
        allowed = allowed.reshape(block_len, (per_block + 2) * block_len)
        scores = (
            jnp.einsum("qhd,kd->hqk", query_here, tiles_k, preferred_element_type=jnp.float32)
            * scale
        )
        scores = jnp.where(allowed[None], scores, -1e30)
        top = jnp.max(scores, axis=2, keepdims=True)
        expo = jnp.exp(scores - top)
        total = jnp.sum(expo, axis=2, keepdims=True)
        weights = (expo / total).astype(jnp.bfloat16)
        result = jnp.einsum("hqk,kd->qhd", weights, tiles_v, preferred_element_type=jnp.float32)
        return result.astype(jnp.bfloat16).reshape(block_len, heads_here * head_size)

    outputs = lax.map(
        attend_block,
        (query_blocks, key_blocks, value_blocks, slot_keys, slot_values, live, numbers),
    )
    return outputs.reshape(blocks_here * block_len, heads_here * head_size)


def solution(mesh):
    in_specs = (P("seq", "head"), P("seq", None), P("seq", None), P("seq", None))
    out_specs = P("seq", "head")
    return jax.shard_map(shards, mesh=mesh, in_specs=in_specs, out_specs=out_specs, check_vma=False)
```

profile of v0, /device:TPU:24, one launch (start us, length us, event | category | flops | bytes accessed | tf_op | source)
XLA Modules:
  0.0 620.2 jit_solution(7477276170318699384)
XLA Ops:
  9.9 12.1 %all-to-all-start = ((s32[64,1,1]{2,1,0:T(1,128)}), s32[64,1,1]{2,1,0:T(1,128)S(1)}, u32[]{:S(2)}, u32[]{:S(2)}) async-start(s32[64,1,1]{2,1,0:T(1,128)} %copy.56), calls=%async_computation | async-start | bytes 65536 | tf_op jit(solution)/shard_map/all_to_all | solution.py:38
  22.0 7.5 %all-to-all-done = s32[64,1,1]{2,1,0:T(1,128)S(1)} async-done(((s32[64,1,1]{2,1,0:T(1,128)}), s32[64,1,1]{2,1,0:T(1,128)S(1)}, u32[]{:S(2)}, u32[]{:S(2)}) %all-to-all-start) | async-done | bytes 288 | tf_op jit(solution)/shard_map/all_to_all | solution.py:38
  29.5 1.2 reduce.5
  30.8 6.4 %gather_fusion = bf16[64,512,128]{2,1,0:T(8,128)(2,1)} fusion(bf16[6,512,128]{2,1,0:T(8,128)(2,1)} %bitcast.90, s32[1024]{0:T(1024)S(1)} %pad_clamp_fusion.2), kind=kCustom, calls=%fused_computation | custom fusion | bytes 16777472 | tf_op jit(solution)/shard_map/gather | solution.py:47
  37.2 7.9 %all-to-all-start.1 = ((bf16[64,512,128]{2,1,0:T(8,128)(2,1)}), bf16[64,512,128]{2,1,0:T(8,128)(2,1)}, u32[]{:S(2)}, u32[]{:S(2)}) async-start(bf16[64,512,128]{2,1,0:T(8,128)(2,1)} %gather_fusion), calls=%async_computation.1 | async-start | bytes 16777216 | tf_op jit(solution)/shard_map/all_to_all | solution.py:47
  45.1 5.3 gather_fusion.3
  50.4 178.1 %all-to-all-done.1 = bf16[64,512,128]{2,1,0:T(8,128)(2,1)} async-done(((bf16[64,512,128]{2,1,0:T(8,128)(2,1)}), bf16[64,512,128]{2,1,0:T(8,128)(2,1)}, u32[]{:S(2)}, u32[]{:S(2)}) %all-to-all-start.1) | async-done | bytes 8388640 | tf_op jit(solution)/shard_map/all_to_all | solution.py:47
  228.5 8.5 %all-to-all-start.2 = ((bf16[64,512,128]{2,1,0:T(8,128)(2,1)}), bf16[64,512,128]{2,1,0:T(8,128)(2,1)}, u32[]{:S(2)}, u32[]{:S(2)}) async-start(bf16[64,512,128]{2,1,0:T(8,128)(2,1)} %gather_fusion.3), calls=%async_computation.2 | async-start | bytes 16777216 | tf_op jit(solution)/shard_map/all_to_all | solution.py:46
  238.7 2.5 gather_fusion.2
  241.2 2.5 gather_fusion.5
  243.8 1.9 reshape.217
  245.7 5.8 gather_fusion.1
  251.5 171.1 %all-to-all-done.2 = bf16[64,512,128]{2,1,0:T(8,128)(2,1)} async-done(((bf16[64,512,128]{2,1,0:T(8,128)(2,1)}), bf16[64,512,128]{2,1,0:T(8,128)(2,1)}, u32[]{:S(2)}, u32[]{:S(2)}) %all-to-all-start.2) | async-done | bytes 8388640 | tf_op jit(solution)/shard_map/all_to_all | solution.py:46
  422.6 5.8 gather_fusion.4
  428.4 6.5 %broadcast_select_fusion = (bf16[6,3,512,128]{3,2,1,0:T(8,128)(2,1)}, bf16[6,3,512,128]{3,2,1,0:T(8,128)(2,1)}) fusion(bf16[6,3,512,128]{3,2,1,0:T(8,128)(2,1)} %bitcast.102, bf16[6,3,512,128]{3,2,1,0:T(8,128)(2,1)} %bitcast.100, pred[6,3]{1,0:T(8,128)(4,1)S(1)} %copy.53, bf16[6,3,512,128]{3,2,1,0:T(8,128)(2,1)} %bitcast.101, ...), kind=kLoop, calls=%fused_computation.38 | loop fusion | flops 2359296 | bytes 14155794 | tf_op jit(solution)/shard_map/jit(_where)/select_n | solution.py:51
  434.9 15.7 %all-reduce.3.cloned.1.call-done = (bf16[512,128]{1,0:T(8,128)(2,1)}, bf16[512,128]{1,0:T(8,128)(2,1)}) async-done(((bf16[512,128]{1,0:T(8,128)(2,1)}, bf16[512,128]{1,0:T(8,128)(2,1)}), (bf16[512,128]{1,0:T(8,128)(2,1)}, bf16[512,128]{1,0:T(8,128)(2,1)})) %all-reduce.3.cloned.1.call-update) | async-done | bytes 262160 | tf_op jit(solution)/shard_map/psum | solution.py:11
  450.6 162.8 %while.14 = (s32[]{:T(128)}, bf16[6,512,256]{2,1,0:T(8,128)(2,1)}, bf16[512,128]{1,0:T(8,128)(2,1)}, bf16[6,512,128]{2,1,0:T(8,128)(2,1)S(1)}, bf16[6,3,512,128]...) while((s32[]{:T(128)}, bf16[6,512,256]{2,1,0:T(8,128)(2,1)}, ...), condition=%wide.region_7.8_spmd.clone, body=%wide.region_4.7_spmd.clone.sunk | while | flops 2038568960 | bytes 34743008 | solution.py:86
  450.6 1.2 dynamic-slice_bitcast_fusion.3
  454.4 1.5 broadcast_in_dim.155
  456.7 1.1 constant_dynamic-slice_fusion.9
  457.8 4.9 fusion.41
  462.7 5.5 fusion.42
  468.3 8.5 %fusion.43 = bf16[128,2,512]{2,0,1:T(8,128)(2,1)S(1)} fusion(bf16[2560,128,1]{1,0,2:T(8,128)(2,1)S(1)} %bitcast.98, f32[2,512]{1,0:T(2,128)S(1)} %fusion.41, f32[2560,512,2]{1,0,2:T(8,128)} %fusion.42, pred[512,2560]{0,1:T(8,128)(4,1)} %bitcast.86), kind=kOutput, calls=%fused_computation.16.clone.1 | convolution fusion | flops 684330496 | bytes 12718080 | tf_op jit(solution)/shard_map/while/body/eval_jaxpr/hqk,kd->qhd/dot_general | solution.py:83
  477.7 1.2 dynamic-slice_bitcast_fusion.3
  481.5 1.5 broadcast_in_dim.155
  484.9 4.9 fusion.41
  489.9 5.5 fusion.42
  495.5 8.5 %fusion.43 = bf16[128,2,512]{2,0,1:T(8,128)(2,1)S(1)} fusion(bf16[2560,128,1]{1,0,2:T(8,128)(2,1)S(1)} %bitcast.98, f32[2,512]{1,0:T(2,128)S(1)} %fusion.41, f32[2560,512,2]{1,0,2:T(8,128)} %fusion.42, pred[512,2560]{0,1:T(8,128)(4,1)} %bitcast.86), kind=kOutput, calls=%fused_computation.16.clone.1 | convolution fusion | flops 684330496 | bytes 12718080 | tf_op jit(solution)/shard_map/while/body/eval_jaxpr/hqk,kd->qhd/dot_general | solution.py:83
  504.9 1.2 dynamic-slice_bitcast_fusion.3
  508.7 1.5 broadcast_in_dim.155
  512.1 4.9 fusion.41
  517.0 5.5 fusion.42
  522.6 8.5 %fusion.43 = bf16[128,2,512]{2,0,1:T(8,128)(2,1)S(1)} fusion(bf16[2560,128,1]{1,0,2:T(8,128)(2,1)S(1)} %bitcast.98, f32[2,512]{1,0:T(2,128)S(1)} %fusion.41, f32[2560,512,2]{1,0,2:T(8,128)} %fusion.42, pred[512,2560]{0,1:T(8,128)(4,1)} %bitcast.86), kind=kOutput, calls=%fused_computation.16.clone.1 | convolution fusion | flops 684330496 | bytes 12718080 | tf_op jit(solution)/shard_map/while/body/eval_jaxpr/hqk,kd->qhd/dot_general | solution.py:83
  532.0 1.2 dynamic-slice_bitcast_fusion.3
  535.8 1.5 broadcast_in_dim.155
  539.2 4.9 fusion.41
  544.2 5.5 fusion.42
  549.7 8.5 %fusion.43 = bf16[128,2,512]{2,0,1:T(8,128)(2,1)S(1)} fusion(bf16[2560,128,1]{1,0,2:T(8,128)(2,1)S(1)} %bitcast.98, f32[2,512]{1,0:T(2,128)S(1)} %fusion.41, f32[2560,512,2]{1,0,2:T(8,128)} %fusion.42, pred[512,2560]{0,1:T(8,128)(4,1)} %bitcast.86), kind=kOutput, calls=%fused_computation.16.clone.1 | convolution fusion | flops 684330496 | bytes 12718080 | tf_op jit(solution)/shard_map/while/body/eval_jaxpr/hqk,kd->qhd/dot_general | solution.py:83
  559.1 1.2 dynamic-slice_bitcast_fusion.3
  562.9 1.5 broadcast_in_dim.155
  566.3 4.9 fusion.41
  571.3 5.5 fusion.42
  576.9 8.5 %fusion.43 = bf16[128,2,512]{2,0,1:T(8,128)(2,1)S(1)} fusion(bf16[2560,128,1]{1,0,2:T(8,128)(2,1)S(1)} %bitcast.98, f32[2,512]{1,0:T(2,128)S(1)} %fusion.41, f32[2560,512,2]{1,0,2:T(8,128)} %fusion.42, pred[512,2560]{0,1:T(8,128)(4,1)} %bitcast.86), kind=kOutput, calls=%fused_computation.16.clone.1 | convolution fusion | flops 684330496 | bytes 12718080 | tf_op jit(solution)/shard_map/while/body/eval_jaxpr/hqk,kd->qhd/dot_general | solution.py:83
  586.3 1.2 dynamic-slice_bitcast_fusion.3
  590.1 1.5 broadcast_in_dim.155
  593.5 4.9 fusion.41
  598.4 5.5 fusion.42
  604.0 8.5 %fusion.43 = bf16[128,2,512]{2,0,1:T(8,128)(2,1)S(1)} fusion(bf16[2560,128,1]{1,0,2:T(8,128)(2,1)S(1)} %bitcast.98, f32[2,512]{1,0:T(2,128)S(1)} %fusion.41, f32[2560,512,2]{1,0,2:T(8,128)} %fusion.42, pred[512,2560]{0,1:T(8,128)(4,1)} %bitcast.86), kind=kOutput, calls=%fused_computation.16.clone.1 | convolution fusion | flops 684330496 | bytes 12718080 | tf_op jit(solution)/shard_map/while/body/eval_jaxpr/hqk,kd->qhd/dot_general | solution.py:83
  (109 shorter events, 32.7 us)
Async XLA Ops:
  9.9 19.6 %all-to-all-start = ((s32[64,1,1]{2,1,0:T(1,128)}), s32[64,1,1]{2,1,0:T(1,128)S(1)}, u32[]{:S(2)}, u32[]{:S(2)}) async-start(s32[64,1,1]{2,1,0:T(1,128)} %copy.56), calls=%async_computation | async-start | bytes 65536 | tf_op jit(solution)/shard_map/all_to_all | solution.py:38
  37.2 8.0 %copy-start.1 = (bf16[3072,128]{1,0:T(8,128)(2,1)S(1)}, bf16[3072,128]{1,0:T(8,128)(2,1)}, u32[]{:S(2)}) copy-start(bf16[3072,128]{1,0:T(8,128)(2,1)} %param.9) | copy-start | bytes 2359300
  37.2 191.3 %all-to-all-start.1 = ((bf16[64,512,128]{2,1,0:T(8,128)(2,1)}), bf16[64,512,128]{2,1,0:T(8,128)(2,1)}, u32[]{:S(2)}, u32[]{:S(2)}) async-start(bf16[64,512,128]{2,1,0:T(8,128)(2,1)} %gather_fusion), calls=%async_computation.1 | async-start | bytes 16777216 | tf_op jit(solution)/shard_map/all_to_all | solution.py:47
  50.4 187.5 %copy-start = (bf16[3072,128]{1,0:T(8,128)(2,1)S(1)}, bf16[3072,128]{1,0:T(8,128)(2,1)}, u32[]{:S(2)}) copy-start(bf16[3072,128]{1,0:T(8,128)(2,1)} %param.10) | copy-start | bytes 2359300
  228.5 194.1 %all-to-all-start.2 = ((bf16[64,512,128]{2,1,0:T(8,128)(2,1)}), bf16[64,512,128]{2,1,0:T(8,128)(2,1)}, u32[]{:S(2)}, u32[]{:S(2)}) async-start(bf16[64,512,128]{2,1,0:T(8,128)(2,1)} %gather_fusion.3), calls=%async_computation.2 | async-start | bytes 16777216 | tf_op jit(solution)/shard_map/all_to_all | solution.py:46
  237.0 213.6 %all-reduce.3.cloned.1.call-start = ((), (), s32[]{:S(2)}) async-start(), calls=%async_computation.3 | async-start | bytes 524288 | tf_op jit(solution)/shard_map/psum | solution.py:11
  241.2 2.6 copy-start.3
  462.7 5.5 copy-start.2
  489.9 5.5 copy-start.2
  517.0 5.5 copy-start.2
  544.1 5.5 copy-start.2
  571.3 5.5 copy-start.2
  598.4 5.5 copy-start.2
Sparse Core Ops, SparseCore 0:
  241.4 209.1 all-reduce.2
where the time goes:
time: 623 us; the launch traced here: 620 us
  waiting for transfers between devices  372 us (60%)
  matrix products  114 us (18%)
  local copies, waits for them, and re-layouts  64.7 us (10%)
  starting transfers between devices  28.8 us (5%)
  other arithmetic  22.7 us (4%)
  between operations  13.5 us (2%)
    all_to_all x1, waiting for transfers between devices, shards(): lax.all_to_all(value_blocks[asked], 'seq', split_axis=0, concat_axis=0, t...  178 us
    all_to_all x1, waiting for transfers between devices, shards(): lax.all_to_all(key_blocks[asked], 'seq', split_axis=0, concat_axis=0, til...  171 us
    dot_general x6, matrix products, attend_block(): jnp.einsum('hqk,kd->qhd', weights, tiles_v, preferred_element_type=jnp.fl...  51.1 us
    dot_general x6, matrix products, attend_block(): jnp.einsum('qhd,kd->hqk', query_here, tiles_k, preferred_element_type=jnp...  33.1 us
    sub x6, matrix products, attend_block(): expo = jnp.exp(scores - top)  29.6 us
    psum x1, waiting for transfers between devices, from_root(): return lax.psum(kept, axis)  15.7 us
  transfers between devices with their start and end apart: 4, of which 4 were waited for; matrix products, arithmetic and copies ran while one was open for 5% of the time, Pallas kernels for 0%

commit v1 on v0

v1 whole, which is shorter than its diff:
```python
import functools
import math

import jax
import jax.numpy as jnp
from jax import lax
from jax.experimental import pallas as pl
from jax.experimental.pallas import tpu as pltpu
from jax.sharding import PartitionSpec as P


def live_slots(chosen):
    nonzero = chosen != 0
    equal = chosen[:, :, None] == chosen[:, None, :]
    order = jnp.arange(chosen.shape[1])
    earlier = order[None, :] < order[:, None]
    repeated = jnp.any(equal & earlier[None, :, :], axis=2)
    return nonzero & jnp.logical_not(repeated)


def attend(blocks, parts, slots, tile_ref, q_ref, k_ref, v_ref, got_ref, out_ref, kt, vt, sc):
    block_len, width = q_ref.shape
    head = k_ref.shape[-1]
    rows = block_len // parts
    null = blocks + slots
    step = pl.program_id(0)

    @pl.when(step == 0)
    def _():
        for b in range(blocks):
            kt[b] = k_ref[b]
            vt[b, :, :head] = v_ref[b]
            vt[b, :, head:] = jnp.ones((block_len, head), jnp.bfloat16)
        for s in range(slots):
            for p in range(parts):
                kt[blocks + s, pl.ds(p * rows, rows)] = got_ref[p, s, 0]
                vt[blocks + s, pl.ds(p * rows, rows), :head] = got_ref[p, s, 1]
            vt[blocks + s, :, head:] = jnp.ones((block_len, head), jnp.bfloat16)
        kt[null] = jnp.broadcast_to(got_ref[0, 0, 0, :1, :], (block_len, head))
        vt[null] = jnp.zeros((block_len, 2 * head), jnp.bfloat16)

    factor = math.log2(math.e) / math.sqrt(head)
    half = block_len // 2
    tiles = [tile_ref[step, j] for j in range(4)]
    for h in range(width // head):
        for r in range(2):
            q = q_ref[pl.ds(r * half, half), pl.ds(h * head, head)]
            own = (r + 1) * half

            def score(keys):
                return lax.dot_general(q, keys, (((1,), (1,)), ((), ())), preferred_element_type=jnp.float32)

            s = score(kt[step, :own])
            row = lax.broadcasted_iota(jnp.int32, (half, own), 0) + r * half
            col = lax.broadcasted_iota(jnp.int32, (half, own), 1)
            s = jnp.where(col <= row, s, -1e30)
            sc[:, :own] = s
            top = jnp.max(s, axis=1, keepdims=True)
            for j in range(4):
                s = score(kt[tiles[j]])
                sc[:, pl.ds((j + 1) * block_len, block_len)] = s
                top = jnp.maximum(top, jnp.max(s, axis=1, keepdims=True))
            shift = top * factor
            p = jnp.exp2(sc[:, :own] * factor - shift).astype(jnp.bfloat16)
            acc = jnp.dot(p, vt[step, :own], preferred_element_type=jnp.float32)
            for j in range(4):
                s = sc[:, pl.ds((j + 1) * block_len, block_len)]
                p = jnp.exp2(s * factor - shift).astype(jnp.bfloat16)
                acc += jnp.dot(p, vt[tiles[j]], preferred_element_type=jnp.float32)
            out = acc[:, :head] / acc[:, head:]
            out_ref[pl.ds(r * half, half), pl.ds(h * head, head)] = out.astype(jnp.bfloat16)


def shards(queries, keys, values, selected):
    seq_count = lax.axis_size("seq")
    parts = lax.axis_size("head")
    me = lax.axis_index("seq")
    blocks, per_block = selected.shape
    head = keys.shape[1]
    block_len = keys.shape[0] // blocks
    rows = block_len // parts
    k3 = keys.reshape(blocks, block_len, head)
    v3 = values.reshape(blocks, block_len, head)
    start = lax.axis_index("head") * rows
    mine = jnp.stack(
        [lax.dynamic_slice_in_dim(k3, start, rows, 1), lax.dynamic_slice_in_dim(v3, start, rows, 1)], axis=1
    )
    owner = (selected // blocks).reshape(-1)
    local = (selected % blocks).reshape(-1)
    remote = owner != me
    owner_list = jnp.arange(seq_count, dtype=jnp.int32)
    hits = (owner[:, None] == owner_list[None, :]) & remote[:, None]
    wanted = jnp.sum(jnp.where(hits, local[:, None], 0), axis=0)
    asked = lax.all_to_all(wanted.reshape(seq_count, 1), "seq", 0, 0, tiled=True).reshape(seq_count)
    zero = lax.psum(jnp.where(me == 0, mine[0], 0).astype(jnp.bfloat16), "seq")
    got = lax.all_to_all(mine[asked], "seq", 0, 0, tiled=True)
    packed = jnp.concatenate([zero[None], got[owner]], axis=0)
    slots = packed.shape[0]
    gathered = lax.all_gather(packed, "head")

    live = live_slots(selected)
    numbers = me * blocks + jnp.arange(blocks, dtype=jnp.int32)
    null = blocks + slots
    place = jnp.where(remote, blocks + 1 + jnp.arange(blocks * per_block, dtype=jnp.int32), local)
    place = jnp.where(live, place.reshape(blocks, per_block), null)
    first = jnp.where(numbers != 0, blocks, null)
    tiles = jnp.concatenate([first[:, None], place], axis=1).astype(jnp.int32)

    whole = lambda *shape: pl.BlockSpec(shape, lambda i, t: (0,) * len(shape))
    return pl.pallas_call(
        functools.partial(attend, blocks, parts, slots),
        out_shape=jax.ShapeDtypeStruct(queries.shape, jnp.bfloat16),
        grid_spec=pltpu.PrefetchScalarGridSpec(
            num_scalar_prefetch=1,
            grid=(blocks,),
            in_specs=[
                pl.BlockSpec((block_len, queries.shape[1]), lambda i, t: (i, 0)),
                whole(*k3.shape),
                whole(*v3.shape),
                whole(*gathered.shape),
            ],
            out_specs=pl.BlockSpec((block_len, queries.shape[1]), lambda i, t: (i, 0)),
            scratch_shapes=[
                pltpu.VMEM((null + 1, block_len, head), jnp.bfloat16),
                pltpu.VMEM((null + 1, block_len, 2 * head), jnp.bfloat16),
                pltpu.VMEM((block_len // 2, 5 * block_len), jnp.float32),
            ],
        ),
        compiler_params=pltpu.CompilerParams(vmem_limit_bytes=48 * 2**20),
    )(tiles, queries, k3, v3, gathered)


def solution(mesh):
    in_specs = (P("seq", "head"), P("seq", None), P("seq", None), P("seq", None))
    return jax.shard_map(shards, mesh=mesh, in_specs=in_specs, out_specs=P("seq", "head"), check_vma=False)
```

time: 623 us -> 323 us (0.52)
  waiting for transfers between devices: 372 us -> 244 us
  matrix products: 114 us -> 0 us
  local copies, waits for them, and re-layouts: 64.7 us -> 9.94 us
  Pallas kernels: 0 us -> 29.8 us
  other arithmetic: 22.7 us -> 5.4 us
  starting transfers between devices: 28.8 us -> 19.7 us
    all_to_all x3 -> x2, waiting for transfers between devices: 357 us -> 100 us  [the longest x1 93.7 us: shards(): got = lax.all_to_all(mine[asked], 'seq', 0, 0, tiled=True)]
    dot_general x12 -> x0, matrix products: 84.2 us -> none  [the longest x6 51.1 us: attend_block(): jnp.einsum('hqk,kd->qhd', weights, tiles_v, preferred_element_type=jnp.fl...]
    psum x1, waiting for transfers between devices: 15.7 us -> 88.8 us  [shards(): zero = lax.psum(jnp.where(me == 0, mine[0], 0).astype(jnp.bfloat16), 'seq')]
    all_gather x0 -> x1, waiting for transfers between devices: none -> 54.8 us  [shards(): gathered = lax.all_gather(packed, 'head')]
    pallas_call x0 -> x1, Pallas kernels: none -> 29.8 us  [shards(): pl.pallas_call(functools.partial(attend, blocks, parts, slots), out_shape...]
    sub x6 -> x0, matrix products: 29.6 us -> none  [attend_block(): expo = jnp.exp(scores - top)]
    gather x6 -> x2, local copies, waits for them, and re-layouts: 28.2 us -> 7.04 us  [the longest x1 3.98 us: shards(): packed = jnp.concatenate([zero[None], got[owner]], axis=0)]
    dynamic_slice x30 -> x0, local copies, waits for them, and re-layouts: 12.1 us -> none  [shards(): lax.map(attend_block, (query_blocks, key_blocks, value_blocks, slot_keys,...]
  transfers between devices with their start and end apart: 4 -> 4, of which waited for: 4 -> 4; matrix products, arithmetic and copies ran while one was open for 5% -> 2% of each run, Pallas kernels for 0% -> 0%
where the time goes in v1:
time: 323 us; the launch traced here: 322 us
  waiting for transfers between devices  244 us (76%)
  Pallas kernels  29.8 us (9%)
  starting transfers between devices  19.7 us (6%)
  between operations  13.5 us (4%)
  local copies, waits for them, and re-layouts  9.94 us (3%)
  other arithmetic  5.4 us (2%)
    all_to_all x1, waiting for transfers between devices, shards(): got = lax.all_to_all(mine[asked], 'seq', 0, 0, tiled=True)  93.7 us
    psum x1, waiting for transfers between devices, shards(): zero = lax.psum(jnp.where(me == 0, mine[0], 0).astype(jnp.bfloat16), 'seq')  88.8 us
    all_gather x1, waiting for transfers between devices, shards(): gathered = lax.all_gather(packed, 'head')  54.8 us
    pallas_call x1, Pallas kernels, shards(): pl.pallas_call(functools.partial(attend, blocks, parts, slots), out_shape...  29.8 us
    all_to_all x1, starting transfers between devices, shards(): lax.all_to_all(wanted.reshape(seq_count, 1), 'seq', 0, 0, tiled=True)  12.1 us
    all_to_all x1, starting transfers between devices, shards(): got = lax.all_to_all(mine[asked], 'seq', 0, 0, tiled=True)  7.51 us
  transfers between devices with their start and end apart: 4, of which 4 were waited for; matrix products, arithmetic and copies ran while one was open for 2% of the time, Pallas kernels for 0%

profile of v1, /device:TPU:24, one launch (start us, length us, event | category | flops | bytes accessed | tf_op | source)
XLA Modules:
  0.0 322.0 jit_solution(14241837579339729179)
XLA Ops:
  6.5 0.8 copy.31
  7.3 0.8 and_reduce_fusion
  8.2 0.1 copy.32
  8.3 0.1 broadcast_in_dim.48
  8.4 0.1 eq.37
  8.5 0.1 select_reduce_fusion
  8.5 0.7 copy.36
  9.3 12.1 %all-to-all-start = ((s32[64,1,1]{2,1,0:T(1,128)}), s32[64,1,1]{2,1,0:T(1,128)S(1)}, u32[]{:S(2)}, u32[]{:S(2)}) async-start(s32[64,1,1]{2,1,0:T(1,128)} %copy.36), calls=%async_computation | async-start | bytes 65536 | tf_op jit(solution)/shard_map/all_to_all | solution.py:94
  21.4 1.1 dynamic-slice_bitcast_fusion
  22.5 6.4 %all-to-all-done = s32[64,1,1]{2,1,0:T(1,128)S(1)} async-done(((s32[64,1,1]{2,1,0:T(1,128)}), s32[64,1,1]{2,1,0:T(1,128)S(1)}, u32[]{:S(2)}, u32[]{:S(2)}) %all-to-all-start) | async-done | bytes 288 | tf_op jit(solution)/shard_map/all_to_all | solution.py:94
  28.9 1.2 reduce
  30.1 3.1 gather_fusion
  33.2 7.5 %all-to-all-start.1 = ((bf16[64,2,128,128]{3,2,1,0:T(8,128)(2,1)}), bf16[64,2,128,128]{3,2,1,0:T(8,128)(2,1)}, u32[]{:S(2)}, u32[]{:S(2)}) async-start(bf16[64,2,128,128]{3,2,1,0:T(8,128)(2,1)} %gather_fusion), calls=%async_computation.1 | async-start | bytes 8388608 | tf_op jit(solution)/shard_map/all_to_all | solution.py:96
  40.7 0.0 all-reduce.2.cloned.1.call-start
  40.7 0.6 fusion.1
  41.4 0.0 all-reduce.2.cloned.1.call-update
  41.4 0.0 all-gather.3.cloned.1.call-start
  41.5 0.1 reshape.111
  41.6 93.7 %all-to-all-done.1 = bf16[64,2,128,128]{3,2,1,0:T(8,128)(2,1)} async-done(((bf16[64,2,128,128]{3,2,1,0:T(8,128)(2,1)}), bf16[64,2,128,128]{3,2,1,0:T(8,128)(2,1)}, u32[]{:S(2)}, u32[]{:S(2)}) %all-to-all-start.1) | async-done | bytes 4194336 | tf_op jit(solution)/shard_map/all_to_all | solution.py:96
  135.3 4.0 %gather_fusion.1 = bf16[18,2,128,128]{3,2,1,0:T(8,128)(2,1)} fusion(bf16[64,2,128,128]{3,2,1,0:T(8,128)(2,1)} %all-to-all-done.1, s32[1024]{0:T(1024)S(1)} %pad_clamp_fusion), kind=kCustom, calls=%fused_computation.1 | custom fusion | bytes 2359368 | tf_op jit(solution)/shard_map/gather | solution.py:97
  139.2 0.0 copy-start
  139.2 0.0 copy-start.1
  139.2 0.0 copy-start.2
  139.3 88.8 %all-reduce.2.cloned.1.call-done = bf16[1,2,128,128]{3,2,1,0:T(8,128)(2,1)} async-done(((bf16[1,2,128,128]{3,2,1,0:T(8,128)(2,1)}), bf16[1,2,128,128]{3,2,1,0:T(8,128)(2,1)}) %all-reduce.2.cloned.1.call-update) | async-done | bytes 65552 | tf_op jit(solution)/shard_map/psum | solution.py:95
  228.1 2.4 pad_maximum_fusion
  230.5 0.0 all-gather.3.cloned.1.call-update
  230.5 0.1 pad_add_fusion.tile_ref
  230.6 54.8 %all-gather.3.cloned.1.call-done = bf16[76,2,128,128]{3,2,1,0:T(8,128)(2,1)} async-done(((bf16[19,2,128,128]{3,2,1,0:T(8,128)(2,1)}), bf16[76,2,128,128]{3,2,1,0:T(8,128)(2,1)}) %all-gather.3.cloned.1.call-update) | async-done | bytes 4980752 | tf_op jit(solution)/shard_map/all_gather | solution.py:99
  285.4 0.0 copy-done
  285.4 0.0 copy-done.1
  285.4 0.0 copy-done.2
  285.4 29.8 %shard_map.46 = bf16[3072,256]{1,0:T(8,128)(2,1)} custom-call(s32[6,4]{1,0:T(8,128)S(1)} %pad_add_fusion.tile_ref, bf16[3072,256]{1,0:T(8,128)(2,1)S(1)} %copy-done, bf16[6,512,128]{2,1,0:T(8,128)(2,1)S(1)} %bitcast.15, bf16[6,512,128]{2,1,0:T(8,128)(2,1)S(1)} %bitcast.17, bf16[4,19,2,128,128]{4,3,2,1,0:T(8,128)(2,1)} %bitcast.18), custom_call_target="tpu_custom_call" | custom-call | tf_op jit(solution)/shard_map/pallas_call | solution.py:110
  (9 shorter events, 0.1 us)
Async XLA Ops:
  9.3 19.6 %all-to-all-start = ((s32[64,1,1]{2,1,0:T(1,128)}), s32[64,1,1]{2,1,0:T(1,128)S(1)}, u32[]{:S(2)}, u32[]{:S(2)}) async-start(s32[64,1,1]{2,1,0:T(1,128)} %copy.36), calls=%async_computation | async-start | bytes 65536 | tf_op jit(solution)/shard_map/all_to_all | solution.py:94
  33.2 102.1 %all-to-all-start.1 = ((bf16[64,2,128,128]{3,2,1,0:T(8,128)(2,1)}), bf16[64,2,128,128]{3,2,1,0:T(8,128)(2,1)}, u32[]{:S(2)}, u32[]{:S(2)}) async-start(bf16[64,2,128,128]{3,2,1,0:T(8,128)(2,1)} %gather_fusion), calls=%async_computation.1 | async-start | bytes 8388608 | tf_op jit(solution)/shard_map/all_to_all | solution.py:96
  40.7 187.4 %all-reduce.2.cloned.1.call-start = ((), (), s32[]{:S(2)}) async-start(), calls=%async_computation.2 | async-start | bytes 131072 | tf_op jit(solution)/shard_map/psum | solution.py:95
  41.4 243.9 %all-gather.3.cloned.1.call-start = ((), (), s32[]{:S(2)}) async-start(), calls=%async_computation.3 | async-start | bytes 6225920 | tf_op jit(solution)/shard_map/all_gather | solution.py:99
  139.2 146.1 %copy-start = (bf16[3072,256]{1,0:T(8,128)(2,1)S(1)}, bf16[3072,256]{1,0:T(8,128)(2,1)}, u32[]{:S(2)}) copy-start(bf16[3072,256]{1,0:T(8,128)(2,1)} %q_ref.1) | copy-start | bytes 4718596
  139.2 146.1 %copy-start.1 = (bf16[3072,128]{1,0:T(8,128)(2,1)S(1)}, bf16[3072,128]{1,0:T(8,128)(2,1)}, u32[]{:S(2)}) copy-start(bf16[3072,128]{1,0:T(8,128)(2,1)} %param.5) | copy-start | bytes 2359300
  139.2 146.1 %copy-start.2 = (bf16[3072,128]{1,0:T(8,128)(2,1)S(1)}, bf16[3072,128]{1,0:T(8,128)(2,1)}, u32[]{:S(2)}) copy-start(bf16[3072,128]{1,0:T(8,128)(2,1)} %param.6) | copy-start | bytes 2359300
Sparse Core Ops, SparseCore 0:
  45.0 183.0 all-reduce.1
  230.6 54.6 all-gather.2

commit v2 on v1

v2 whole, which is shorter than its diff:
```python
import functools
import math

import jax
import jax.numpy as jnp
from jax import lax
from jax.experimental import pallas as pl
from jax.experimental.pallas import tpu as pltpu
from jax.sharding import PartitionSpec as P

MESH = pl.DeviceIdType.MESH
NY, NZ, NC, NX = 4, 8, 2, 4
GROUPS = 8
SPAN = 9
ARRIVAL = ((0,), (7, 1), (6, 2), (5, 3), (4,))
PLACE = (0, 2, 4, 6, 7, 5, 3, 1)


def live_slots(chosen):
    nonzero = chosen != 0
    equal = chosen[:, :, None] == chosen[:, None, :]
    order = jnp.arange(chosen.shape[1])
    earlier = order[None, :] < order[:, None]
    repeated = jnp.any(equal & earlier[None, :, :], axis=2)
    return nonzero & jnp.logical_not(repeated)


def exchange(blocks, rows, slots, source_ref, want_smem, want_ref, k_hbm, v_hbm, gk_hbm, gv_hbm, *scratch):
    zs = (scratch[0:8], scratch[8:16])
    sp = scratch[16:18]
    rp = scratch[18:20]
    zero = scratch[20:22]
    xs = scratch[22:24]
    (tabs, tabs_smem, local_sem, tab_local, zsend, zrecv, ysend, yrecv, nsend, nrecv,
     tsend, trecv, xsend, xrecv, xlocal) = scratch[24:]
    hbm = (k_hbm, v_hbm)
    outs = (gk_hbm, gv_hbm)
    s = lax.axis_index("seq")
    x = lax.axis_index("head")
    c = lax.rem(s, NC)
    z = lax.rem(s // NC, NZ)
    y = s // (NC * NZ)

    def at(y2, z2, c2):
        return ((y2 * NZ + z2) * NC + c2, x)

    zr, zl = lax.rem(z + 1, NZ), lax.rem(z + NZ - 1, NZ)
    xr, xl = lax.rem(x + 1, NX), lax.rem(x + NX - 1, NX)
    right, left = at(y, zr, c), at(y, zl, c)
    other = at(y, z, 1 - c)
    x_right, x_left = (s, xr), (s, xl)
    mine = pl.ds(pl.multiple_of(x * rows, rows), rows)

    def remote(src, dst, ss, rs, dev):
        return pltpu.make_async_remote_copy(
            src_ref=src, dst_ref=dst, send_sem=ss, recv_sem=rs, device_id=dev, device_id_type=MESH
        )

    loads = [pltpu.make_async_copy(hbm[p].at[:, mine, :], zs[p][0], local_sem.at[p]) for p in range(2)]
    for copy in loads:
        copy.start()

    barrier = pltpu.get_barrier_semaphore()
    partners = [right, left, other, x_right, x_left]
    for dy in range(1, NY):
        for c2 in range(NC):
            partners.append(at(lax.rem(y + dy, NY), z, c2))
    for dev in partners:
        pl.semaphore_signal(barrier, inc=1, device_id=dev, device_id_type=MESH)
    for copy in loads:
        copy.wait()
    pl.semaphore_wait(barrier, len(partners))

    def z_copies(p, k):
        if k < 4:
            a = remote(zs[p][(9 - k) % 8], zs[p][8 - k], zsend.at[p, k - 1, 0], zrecv.at[p, k - 1, 0], right)
            b = remote(zs[p][k - 1], zs[p][k], zsend.at[p, k - 1, 1], zrecv.at[p, k - 1, 1], left)
        else:
            lo, hi = pl.ds(0, blocks // 2), pl.ds(blocks // 2, blocks - blocks // 2)
            a = remote(zs[p][5].at[lo], zs[p][4].at[lo], zsend.at[p, 3, 0], zrecv.at[p, 3, 0], right)
            b = remote(zs[p][3].at[hi], zs[p][4].at[hi], zsend.at[p, 3, 1], zrecv.at[p, 3, 1], left)
        return a, b

    def z_start(p, k):
        for copy in z_copies(p, k):
            copy.start()

    def z_wait(p, k):
        for copy in z_copies(p, k):
            copy.wait_recv()

    z_start(0, 1)

    def table(g_there, sem, dev):
        return remote(want_ref, tabs.at[g_there], tsend.at[sem], trecv.at[g_there], dev)

    def table_in(g):
        return pltpu.make_async_copy(tabs.at[g], tabs_smem.at[g], tab_local.at[g])

    table(0, 0, other).start()
    for dy in range(1, NY):
        @pl.when(y >= dy)
        def _():
            for c2 in range(NC):
                table(2 * dy - 1 + c, 2 * dy - 1 + c2, at(y - dy, z, c2)).start()
    table(0, 0, other).wait_recv()
    table_in(0).start()
    for dy in range(1, NY):
        @pl.when(y + dy < NY)
        def _():
            for c2 in range(NC):
                g = 2 * dy - 1 + c2
                table(g, g, other).wait_recv()
                table_in(g).start()
    table_in(0).wait()
    for dy in range(1, NY):
        @pl.when(y + dy < NY)
        def _():
            for c2 in range(NC):
                table_in(2 * dy - 1 + c2).wait()

    def y_copy(p, g_here, g_there, place, dev):
        return remote(
            sp[p].at[pl.ds(g_here * SPAN + place[0], place[1])],
            rp[p].at[pl.ds(g_there * SPAN + place[0], place[1])],
            ysend.at[p, g_here], yrecv.at[p, g_there], dev,
        )

    starts = (0, 1, 3, 5, 7)

    def owner_at(d):
        return (y * NZ + lax.rem(z + d, NZ)) * NC + c

    def push(p, k):
        place = (starts[k], len(ARRIVAL[k]))

        def pack(g):
            for j, d in enumerate(ARRIVAL[k]):
                sp[p][g * SPAN + place[0] + j] = zs[p][d][tabs_smem[g, 0, owner_at(d)]]

        for dy in (2, 1, 3):
            @pl.when(y + dy < NY)
            def _():
                for c2 in range(NC):
                    g = 2 * dy - 1 + c2
                    pack(g)
                    y_copy(p, g, 2 * dy - 1 + c, place, at(y + dy, z, c2)).start()
        pack(0)
        y_copy(p, 0, 0, place, other).start()
        for j, d in enumerate(ARRIVAL[k]):
            rp[p][7 * SPAN + place[0] + j] = zs[p][d][want_smem[0, owner_at(d)]]
        for d in ARRIVAL[k]:
            @pl.when((y == 0) & (c == 0) & (z == (8 - d) % 8))
            def _():
                zero[p][...] = zs[p][d][0]

    def n_copy(p, g_there, sem, dev):
        return remote(zero[p], rp[p].at[g_there * SPAN + 8], nsend.at[p, sem], nrecv.at[p], dev)

    def push_zero(p):
        @pl.when((y == 0) & (c == 0))
        def _():
            for dy in range(1, NY):
                for c2 in range(NC):
                    g = 2 * dy - 1 + c2
                    n_copy(p, 2 * dy - 1, g, at(dy, z, c2)).start()
            n_copy(p, 0, 0, other).start()
            rp[p][7 * SPAN + 8] = zero[p][...]

    def y_wait(p):
        whole = (0, 8)
        y_copy(p, 0, 0, whole, other).wait_recv()
        for dy in range(1, NY):
            @pl.when(y >= dy)
            def _():
                for c2 in range(NC):
                    g = 2 * dy - 1 + c2
                    y_copy(p, g, g, whole, other).wait_recv()
                    if c2 == 0:
                        @pl.when(y == dy)
                        def _():
                            n_copy(p, g, g, other).wait_recv()
        @pl.when((y == 0) & (c == 1))
        def _():
            n_copy(p, 0, 0, other).wait_recv()

    cut = (slots + 1) // 2
    first, second = pl.ds(0, cut), pl.ds(cut, slots - cut)

    def compact(p):
        zero_group = jnp.where(y == 0, jnp.where(c == 0, 7, 0), 2 * y - 1)
        xs[p][0] = rp[p][zero_group * SPAN + 8]
        for j in range(slots - 1):
            xs[p][j + 1] = rp[p][source_ref[j]]

    def quarter(of):
        return pl.ds(pl.multiple_of(of * rows, rows), rows)

    def x_direct(p, part, way):
        sem = 2 * way + part
        span = (first, second)[part]
        return remote(
            xs[p].at[span], outs[p].at[span, mine, :],
            xsend.at[p, sem], xrecv.at[p, sem], (x_right, x_left)[way],
        )

    def x_direct_in(p, part, way):
        sem = 2 * way + part
        span = (first, second)[part]
        return remote(
            xs[p].at[span], outs[p].at[span, quarter((xl, xr)[way]), :],
            xsend.at[p, sem], xrecv.at[p, sem], (x_right, x_left)[way],
        )

    def x_relay(p, way):
        span = (first, second)[way]
        region = outs[p].at[span, quarter((xl, xr)[way]), :]
        return remote(region, region, xsend.at[p, 4 + way], xrecv.at[p, 4 + way], (x_right, x_left)[way])

    def x_relay_in(p, way):
        span = (first, second)[way]
        region = outs[p].at[span, quarter(lax.rem(x + 2, NX)), :]
        return remote(region, region, xsend.at[p, 4 + way], xrecv.at[p, 4 + way], (x_right, x_left)[way])

    def x_own(p):
        return pltpu.make_async_copy(xs[p], outs[p].at[:, mine, :], xlocal.at[p])

    def x_start(p):
        x_direct(p, 0, 0).start()
        x_direct(p, 1, 1).start()
        x_direct(p, 1, 0).start()
        x_direct(p, 0, 1).start()
        x_own(p).start()

    def x_forward(p):
        x_direct_in(p, 0, 0).wait_recv()
        x_relay(p, 0).start()
        x_direct_in(p, 1, 1).wait_recv()
        x_relay(p, 1).start()

    def x_finish(p):
        x_direct_in(p, 1, 0).wait_recv()
        x_direct_in(p, 0, 1).wait_recv()
        x_relay_in(p, 0).wait_recv()
        x_relay_in(p, 1).wait_recv()
        x_own(p).wait()

    push(0, 0)
    for k in range(1, 5):
        z_wait(0, k)
        if k < 4:
            z_start(0, k + 1)
        else:
            z_start(1, 1)
        push(0, k)
    push_zero(0)
    push(1, 0)
    z_wait(1, 1)
    z_start(1, 2)
    push(1, 1)
    y_wait(0)
    compact(0)
    x_start(0)
    z_wait(1, 2)
    z_start(1, 3)
    push(1, 2)
    z_wait(1, 3)
    z_start(1, 4)
    push(1, 3)
    x_forward(0)
    z_wait(1, 4)
    push(1, 4)
    push_zero(1)
    y_wait(1)
    compact(1)
    x_start(1)
    x_finish(0)
    x_forward(1)
    x_finish(1)

    for p in range(2):
        for k in range(1, 5):
            for copy in z_copies(p, k):
                copy.wait_send()
        whole = (0, 8)
        y_copy(p, 0, 0, whole, other).wait_send()
        for dy in range(1, NY):
            @pl.when(y + dy < NY)
            def _():
                for c2 in range(NC):
                    g = 2 * dy - 1 + c2
                    y_copy(p, g, g, whole, other).wait_send()
        @pl.when((y == 0) & (c == 0))
        def _():
            for g in range(7):
                n_copy(p, 0, g, other).wait_send()
        for part in range(2):
            for way in range(2):
                x_direct(p, part, way).wait_send()
        for way in range(2):
            x_relay(p, way).wait_send()
    table(0, 0, other).wait_send()
    for dy in range(1, NY):
        @pl.when(y >= dy)
        def _():
            for c2 in range(NC):
                table(0, 2 * dy - 1 + c2, other).wait_send()


def attend(blocks, slots, tile_ref, q_ref, k_hbm, v_hbm, gk_hbm, gv_hbm, out_ref, kt, vt, sc, sem):
    block_len, width = q_ref.shape
    head = kt.shape[-1]
    null = blocks + slots
    step = pl.program_id(0)

    @pl.when(step == 0)
    def _():
        copies = [
            pltpu.make_async_copy(k_hbm, kt.at[pl.ds(0, blocks)], sem.at[0]),
            pltpu.make_async_copy(v_hbm, vt.at[pl.ds(0, blocks), :, pl.ds(0, head)], sem.at[1]),
            pltpu.make_async_copy(gk_hbm, kt.at[pl.ds(blocks, slots)], sem.at[2]),
            pltpu.make_async_copy(gv_hbm, vt.at[pl.ds(blocks, slots), :, pl.ds(0, head)], sem.at[3]),
        ]
        for copy in copies:
            copy.start()
        for t in range(null):
            vt[t, :, head:] = jnp.ones((block_len, head), jnp.bfloat16)
        vt[null] = jnp.zeros((block_len, 2 * head), jnp.bfloat16)
        for copy in copies:
            copy.wait()
        kt[null] = jnp.broadcast_to(kt[blocks, :1, :], (block_len, head))

    factor = math.log2(math.e) / math.sqrt(head)
    half = block_len // 2
    tiles = [tile_ref[step, j] for j in range(4)]
    for h in range(width // head):
        for r in range(2):
            q = q_ref[pl.ds(r * half, half), pl.ds(h * head, head)]
            own = (r + 1) * half

            def score(keys):
                return lax.dot_general(q, keys, (((1,), (1,)), ((), ())), preferred_element_type=jnp.float32)

            s = score(kt[step, :own])
            row = lax.broadcasted_iota(jnp.int32, (half, own), 0) + r * half
            col = lax.broadcasted_iota(jnp.int32, (half, own), 1)
            s = jnp.where(col <= row, s, -1e30)
            sc[:, :own] = s
            top = jnp.max(s, axis=1, keepdims=True)
            for j in range(4):
                s = score(kt[tiles[j]])
                sc[:, pl.ds((j + 1) * block_len, block_len)] = s
                top = jnp.maximum(top, jnp.max(s, axis=1, keepdims=True))
            shift = top * factor
            p = jnp.exp2(sc[:, :own] * factor - shift).astype(jnp.bfloat16)
            acc = jnp.dot(p, vt[step, :own], preferred_element_type=jnp.float32)
            for j in range(4):
                s = sc[:, pl.ds((j + 1) * block_len, block_len)]
                p = jnp.exp2(s * factor - shift).astype(jnp.bfloat16)
                acc += jnp.dot(p, vt[tiles[j]], preferred_element_type=jnp.float32)
            out = acc[:, :head] / acc[:, head:]
            out_ref[pl.ds(r * half, half), pl.ds(h * head, head)] = out.astype(jnp.bfloat16)


def shards(queries, keys, values, selected):
    me = lax.axis_index("seq")
    blocks, per_block = selected.shape
    head = keys.shape[1]
    block_len = keys.shape[0] // blocks
    rows = block_len // NX
    slots = blocks * per_block + 1
    k3 = keys.reshape(blocks, block_len, head)
    v3 = values.reshape(blocks, block_len, head)

    owner = (selected // blocks).reshape(-1)
    local = (selected % blocks).reshape(-1)
    remote = owner != me
    hits = (owner[:, None] == jnp.arange(128, dtype=jnp.int32)[None, :]) & remote[:, None]
    want = jnp.sum(jnp.where(hits, local[:, None], 0), axis=0).astype(jnp.int32)
    want = jnp.broadcast_to(want[None, :], (8, 128))
    y, z, c = me // (NZ * NC), (me // NC) % NZ, me % NC
    oy, oz, oc = owner // (NZ * NC), (owner // NC) % NZ, owner % NC
    dy, dz = y - oy, (oz - z) % NZ
    group = jnp.where(dy == 0, jnp.where(oc == c, 7, 0), 2 * dy - 1 + oc)
    place = jnp.where(dz <= 4, jnp.where(dz == 4, 7, 2 * dz), 2 * (NZ - dz) - 1)
    live = live_slots(selected).reshape(-1)
    source = jnp.where(live & remote, group * SPAN + place, 7 * SPAN).astype(jnp.int32)

    part = lambda *shape: pltpu.VMEM(shape + (rows, head), jnp.bfloat16)
    smem = pl.BlockSpec(memory_space=pltpu.SMEM)
    hbm = pl.BlockSpec(memory_space=pl.ANY)
    dma = pltpu.SemaphoreType.DMA
    got = jax.ShapeDtypeStruct((slots, block_len, head), jnp.bfloat16)
    gk, gv = pl.pallas_call(
        functools.partial(exchange, blocks, rows, slots),
        out_shape=(got, got),
        in_specs=[smem, smem, pl.BlockSpec(memory_space=pltpu.VMEM), hbm, hbm],
        out_specs=(hbm, hbm),
        scratch_shapes=[part(blocks)] * 16
        + [part(7 * SPAN)] * 2
        + [part(GROUPS * SPAN)] * 2
        + [part()] * 2
        + [part(slots)] * 2
        + [
            pltpu.VMEM((7, 8, 128), jnp.int32), pltpu.SMEM((7, 8, 128), jnp.int32),
            dma((2,)), dma((7,)),
            dma((2, 4, 2)), dma((2, 4, 2)), dma((2, 7)), dma((2, 7)), dma((2, 7)), dma((2,)),
            dma((7,)), dma((7,)), dma((2, 6)), dma((2, 6)), dma((2,)),
        ],
        compiler_params=pltpu.CompilerParams(
            collective_id=0, has_side_effects=True, vmem_limit_bytes=40 * 2**20
        ),
    )(source, want, want, k3, v3)

    numbers = me * blocks + jnp.arange(blocks, dtype=jnp.int32)
    null = blocks + slots
    tile = jnp.where(remote, blocks + 1 + jnp.arange(blocks * per_block, dtype=jnp.int32), local)
    tile = jnp.where(live, tile, null).reshape(blocks, per_block)
    front = jnp.where(numbers != 0, blocks, null)
    tiles = jnp.concatenate([front[:, None], tile], axis=1).astype(jnp.int32)

    return pl.pallas_call(
        functools.partial(attend, blocks, slots),
        out_shape=jax.ShapeDtypeStruct(queries.shape, jnp.bfloat16),
        grid_spec=pltpu.PrefetchScalarGridSpec(
            num_scalar_prefetch=1,
            grid=(blocks,),
            in_specs=[pl.BlockSpec((block_len, queries.shape[1]), lambda i, t: (i, 0)), hbm, hbm, hbm, hbm],
            out_specs=pl.BlockSpec((block_len, queries.shape[1]), lambda i, t: (i, 0)),
            scratch_shapes=[
                pltpu.VMEM((null + 1, block_len, head), jnp.bfloat16),
                pltpu.VMEM((null + 1, block_len, 2 * head), jnp.bfloat16),
                pltpu.VMEM((block_len // 2, 5 * block_len), jnp.float32),
                dma((4,)),
            ],
        ),
        compiler_params=pltpu.CompilerParams(vmem_limit_bytes=40 * 2**20),
    )(tiles, queries, k3, v3, gk, gv)


def solution(mesh):
    in_specs = (P("seq", "head"), P("seq", None), P("seq", None), P("seq", None))
    return jax.shard_map(shards, mesh=mesh, in_specs=in_specs, out_specs=P("seq", "head"), check_vma=False)
```

time: 323 us -> 122 us (0.38)
  waiting for transfers between devices: 244 us -> 0 us
  Pallas kernels: 29.8 us -> 114 us
  starting transfers between devices: 19.7 us -> 0 us
  between operations: 13.5 us -> 0.06 us
  other arithmetic: 5.4 us -> 1.09 us
  local copies, waits for them, and re-layouts: 9.94 us -> 5.65 us
    all_to_all x2 -> x0, waiting for transfers between devices: 100 us -> none  [the longest x1 93.7 us: shards(): got = lax.all_to_all(mine[asked], 'seq', 0, 0, tiled=True)]
    psum x1 -> x0, waiting for transfers between devices: 88.8 us -> none  [shards(): zero = lax.psum(jnp.where(me == 0, mine[0], 0).astype(jnp.bfloat16), 'seq')]
    pallas_call x1 -> x2, Pallas kernels: 29.8 us -> 114 us  [the longest x1 85.8 us: shards(): pl.pallas_call(functools.partial(exchange, blocks, rows, slots), out_shap...]
    all_gather x1 -> x0, waiting for transfers between devices: 54.8 us -> none  [shards(): gathered = lax.all_gather(packed, 'head')]
    all_to_all x2 -> x0, starting transfers between devices: 19.6 us -> none  [the longest x1 12.1 us: shards(): lax.all_to_all(wanted.reshape(seq_count, 1), 'seq', 0, 0, tiled=True)]
    gather x2 -> x0, local copies, waits for them, and re-layouts: 7.04 us -> none  [the longest x1 3.98 us: shards(): packed = jnp.concatenate([zero[None], got[owner]], axis=0)]
    unnamed x7 -> x11, local copies, waits for them, and re-layouts: 0.78 us -> 5.29 us
  transfers between devices with their start and end apart: 4 -> 0, of which waited for: 4 -> 0; matrix products, arithmetic and copies ran while one was open for 2% -> 0% of each run, Pallas kernels for 0% -> 0%
where the time goes in v2:
time: 122 us; the launch traced here: 120 us
  Pallas kernels  114 us (93%)
  local copies, waits for them, and re-layouts  5.65 us (5%)
    pallas_call x1, Pallas kernels, shards(): pl.pallas_call(functools.partial(exchange, blocks, rows, slots), out_shap...  85.8 us
    pallas_call x1, Pallas kernels, shards(): pl.pallas_call(functools.partial(attend, blocks, slots), out_shape=jax.Sh...  27.9 us
    unnamed x11, local copies, waits for them, and re-layouts  5.29 us

profile of v2, /device:TPU:24, one launch (start us, length us, event | category | flops | bytes accessed | tf_op | source)
XLA Modules:
  0.0 120.5 jit_solution(13720881608366365558)
XLA Ops:
  0.0 0.8 and_reduce_fusion
  0.9 0.1 copy.18
  1.0 0.8 copy.17
  1.8 0.1 pad_add_fusion.tile_ref
  1.8 0.1 broadcast_in_dim.53
  1.9 0.1 reshape.53
  2.0 0.1 select_reduce_fusion
  2.1 0.1 reshape.52
  2.2 0.0 copy-start
  2.2 1.1 copy-done
  3.4 0.0 copy-start.2
  3.4 1.1 copy-done.2
  4.5 0.0 copy-start.4
  4.5 85.8 %shard_map.46 = (bf16[19,512,128]{2,1,0:T(8,128)(2,1)S(1)}, bf16[19,512,128]{2,1,0:T(8,128)(2,1)S(1)}) custom-call(s32[18]{0:T(128)S(1)} %and_select_fusion.5.source_ref, s32[8,128]{1,0:T(8,128)S(1)} %broadcast_in_dim.56.want_smem.want_ref, s32[8,128]{1,0:T(8,128)S(1)} %broadcast_in_dim.56.want_smem.want_ref, bf16[6,512,128]{2,1,0:T(8,128)(2,1)S(1)} %bitcast.2, ...), custom_call_target="tpu_custom_call" | custom-call | tf_op jit(solution)/shard_map/pallas_call | solution.py:394
  90.3 0.0 copy-done.4
  90.3 0.0 copy-start.1
  90.3 1.1 copy-done.1
  91.4 0.0 copy-start.3
  91.4 1.1 copy-done.3
  92.5 27.9 %shard_map.47 = bf16[3072,256]{1,0:T(8,128)(2,1)} custom-call(s32[6,4]{1,0:T(8,128)S(1)} %pad_add_fusion.tile_ref, bf16[3072,256]{1,0:T(8,128)(2,1)S(1)} %copy-done.4, bf16[6,512,128]{2,1,0:T(8,128)(2,1)S(1)} %bitcast.3, bf16[6,512,128]{2,1,0:T(8,128)(2,1)S(1)} %bitcast.5, bf16[19,512,128]{2,1,0:T(8,128)(2,1)S(1)} %get-tuple-element.7.gk_hbm, ...), custom_call_target="tpu_custom_call" | custom-call | tf_op jit(solution)/shard_map/pallas_call | solution.py:422
  (6 shorter events, 0.1 us)
Async XLA Ops:
  2.2 1.1 copy-start
  3.4 1.1 copy-start.2
  4.5 85.8 %copy-start.4 = (bf16[3072,256]{1,0:T(8,128)(2,1)S(1)}, bf16[3072,256]{1,0:T(8,128)(2,1)}, u32[]{:S(2)}) copy-start(bf16[3072,256]{1,0:T(8,128)(2,1)} %q_ref.1) | copy-start | bytes 4718596
  90.3 1.1 copy-start.1
  91.4 1.1 copy-start.3

commit v3 on v2

v3 whole, which is shorter than its diff:
```python
import functools
import math

import jax
import jax.numpy as jnp
from jax import lax
from jax.experimental import pallas as pl
from jax.experimental.pallas import tpu as pltpu
from jax.sharding import PartitionSpec as P

MESH = pl.DeviceIdType.MESH
NY, NZ, NC, NX = 4, 8, 2, 4
GROUPS = 8
SPAN = 9
ARRIVAL = ((0,), (7, 1), (6, 2), (5, 3), (4,))
STARTS = (0, 1, 3, 5, 7)
PARTS = 4


def fused(blocks, picks, block_len, heads, sel, q_hbm, k_hbm, v_hbm, out_hbm, *scratch):
    rows = block_len // (2 * NX)
    half = block_len // 2
    head = k_hbm.shape[-1]
    slots = blocks * picks + 1
    null = blocks + slots
    zs = [scratch[8 * p:8 * p + 8] for p in range(PARTS)]
    sp = scratch[32:36]
    rp = scratch[36:40]
    zero = scratch[40:44]
    tiles = scratch[44:48]
    (q_vm, k_vm, v_vm, out_vm, prob, sc, m_ref, l_ref, acc_ref, want_ref,
     tabs, tabs_smem, load_sem, tab_local, zsend, zrecv, ysend, yrecv, nsend, nrecv,
     tsend, trecv, xsend, xrecv, out_sem) = scratch[48:]
    s = lax.axis_index("seq")
    x = lax.axis_index("head")
    c = lax.rem(s, NC)
    z = lax.rem(s // NC, NZ)
    y = s // (NC * NZ)

    def at(y2, z2, c2):
        return ((y2 * NZ + z2) * NC + c2, x)

    zr, zl = lax.rem(z + 1, NZ), lax.rem(z + NZ - 1, NZ)
    xr, xl, xo = lax.rem(x + 1, NX), lax.rem(x + NX - 1, NX), lax.rem(x + 2, NX)
    right, left = at(y, zr, c), at(y, zl, c)
    other = at(y, z, 1 - c)
    x_right, x_left = (s, xr), (s, xl)

    def remote(src, dst, ss, rs, dev):
        return pltpu.make_async_remote_copy(
            src_ref=src, dst_ref=dst, send_sem=ss, recv_sem=rs, device_id=dev, device_id_type=MESH
        )

    def source(p):
        return (k_hbm, v_hbm)[p % 2]

    loads = [pltpu.make_async_copy(source(p).at[:, x, p // 2], zs[p][0], load_sem.at[p]) for p in range(PARTS)]
    for p in range(PARTS):
        loads.append(
            pltpu.make_async_copy(
                source(p).at[:, :, p // 2], tiles[p].at[pl.ds(0, blocks)], load_sem.at[PARTS + p]
            )
        )
    loads.append(pltpu.make_async_copy(k_hbm, k_vm, load_sem.at[8]))
    loads.append(pltpu.make_async_copy(v_hbm, v_vm, load_sem.at[9]))
    loads.append(pltpu.make_async_copy(q_hbm, q_vm, load_sem.at[10]))
    for copy in loads:
        copy.start()

    barrier = pltpu.get_barrier_semaphore()
    partners = [right, left, other, x_right, x_left]
    for dy in range(1, NY):
        for c2 in range(NC):
            partners.append(at(lax.rem(y + dy, NY), z, c2))
    for dev in partners:
        pl.semaphore_signal(barrier, inc=1, device_id=dev, device_id_type=MESH)

    lane = lax.broadcasted_iota(jnp.int32, (8, 128), 1)
    want = jnp.zeros((8, 128), jnp.int32)
    for b in range(blocks):
        for j in range(picks):
            chosen = sel[b, j]
            owner = jnp.where(chosen != 0, chosen // blocks, -1)
            want = jnp.where(lane == owner, lax.rem(chosen, blocks), want)
    want_ref[...] = jnp.where(lane == s, 0, want)
    own_table = pltpu.make_async_copy(want_ref, tabs_smem.at[7], tab_local.at[7])
    own_table.start()

    def live(b, j):
        chosen = sel[b, j]
        ok = chosen != 0
        for i in range(j):
            ok = ok & (chosen != sel[b, i])
        return ok

    def slot_source(b, j):
        owner = sel[b, j] // blocks
        oy, oz, oc = owner // (NZ * NC), lax.rem(owner // NC, NZ), lax.rem(owner, NC)
        dy, dz = y - oy, lax.rem(oz - z + NZ, NZ)
        group = jnp.where(dy == 0, jnp.where(oc == c, 7, 0), 2 * dy - 1 + oc)
        place = jnp.where(dz < 4, 2 * dz, jnp.where(dz == 4, 7, 2 * (NZ - dz) - 1))
        return jnp.where(live(b, j) & (owner != s), group * SPAN + place, 7 * SPAN)

    def tile_of(b, j):
        if j == 0:
            return jnp.where(s * blocks + b != 0, blocks, null)
        chosen = sel[b, j - 1]
        here = jnp.where(chosen // blocks == s, lax.rem(chosen, blocks), blocks + 1 + b * picks + (j - 1))
        return jnp.where(live(b, j - 1), here, null)

    for copy in loads[:PARTS]:
        copy.wait()
    pl.semaphore_wait(barrier, len(partners))

    def z_copies(p, k):
        if k < 4:
            a = remote(zs[p][(9 - k) % 8], zs[p][8 - k], zsend.at[p, k - 1, 0], zrecv.at[p, k - 1, 0], right)
            b = remote(zs[p][k - 1], zs[p][k], zsend.at[p, k - 1, 1], zrecv.at[p, k - 1, 1], left)
        else:
            lo, hi = pl.ds(0, blocks // 2), pl.ds(blocks // 2, blocks - blocks // 2)
            a = remote(zs[p][5].at[lo], zs[p][4].at[lo], zsend.at[p, 3, 0], zrecv.at[p, 3, 0], right)
            b = remote(zs[p][3].at[hi], zs[p][4].at[hi], zsend.at[p, 3, 1], zrecv.at[p, 3, 1], left)
        return a, b

    def z_start(p, k):
        for copy in z_copies(p, k):
            copy.start()

    def z_wait(p, k):
        for copy in z_copies(p, k):
            copy.wait_recv()

    z_start(0, 1)

    def table(g_there, sem, dev):
        return remote(want_ref, tabs.at[g_there], tsend.at[sem], trecv.at[g_there], dev)

    def table_in(g):
        return pltpu.make_async_copy(tabs.at[g], tabs_smem.at[g], tab_local.at[g])

    table(0, 0, other).start()
    for dy in range(1, NY):
        @pl.when(y >= dy)
        def _():
            for c2 in range(NC):
                table(2 * dy - 1 + c, 2 * dy - 1 + c2, at(y - dy, z, c2)).start()
    table(0, 0, other).wait_recv()
    table_in(0).start()
    for dy in range(1, NY):
        @pl.when(y + dy < NY)
        def _():
            for c2 in range(NC):
                g = 2 * dy - 1 + c2
                table(g, g, other).wait_recv()
                table_in(g).start()
    table_in(0).wait()
    for dy in range(1, NY):
        @pl.when(y + dy < NY)
        def _():
            for c2 in range(NC):
                table_in(2 * dy - 1 + c2).wait()
    own_table.wait()

    def y_copy(p, g_here, g_there, place, dev):
        return remote(
            sp[p].at[pl.ds(g_here * SPAN + place[0], place[1])],
            rp[p].at[pl.ds(g_there * SPAN + place[0], place[1])],
            ysend.at[p, g_here], yrecv.at[p, g_there], dev,
        )

    def owner_at(d):
        return (y * NZ + lax.rem(z + d, NZ)) * NC + c

    def push(p, k):
        place = (STARTS[k], len(ARRIVAL[k]))

        def pack(g):
            for j, d in enumerate(ARRIVAL[k]):
                sp[p][g * SPAN + place[0] + j] = zs[p][d][tabs_smem[g, 0, owner_at(d)]]

        for dy in (2, 1, 3):
            @pl.when(y + dy < NY)
            def _():
                for c2 in range(NC):
                    g = 2 * dy - 1 + c2
                    pack(g)
                    y_copy(p, g, 2 * dy - 1 + c, place, at(y + dy, z, c2)).start()
        pack(0)
        y_copy(p, 0, 0, place, other).start()
        for j, d in enumerate(ARRIVAL[k]):
            rp[p][7 * SPAN + place[0] + j] = zs[p][d][tabs_smem[7, 0, owner_at(d)]]
        for d in ARRIVAL[k]:
            @pl.when((y == 0) & (c == 0) & (z == (8 - d) % 8))
            def _():
                zero[p][...] = zs[p][d][0]
        if k == 4:
            push_zero(p)

    def n_copy(p, g_there, sem, dev):
        return remote(zero[p], rp[p].at[g_there * SPAN + 8], nsend.at[p, sem], nrecv.at[p], dev)

    def push_zero(p):
        @pl.when((y == 0) & (c == 0))
        def _():
            for dy in range(1, NY):
                for c2 in range(NC):
                    g = 2 * dy - 1 + c2
                    n_copy(p, 2 * dy - 1, g, at(dy, z, c2)).start()
            n_copy(p, 0, 0, other).start()
            rp[p][7 * SPAN + 8] = zero[p][...]

    def y_wait(p):
        whole = (0, 8)
        y_copy(p, 0, 0, whole, other).wait_recv()
        for dy in range(1, NY):
            @pl.when(y >= dy)
            def _():
                for c2 in range(NC):
                    g = 2 * dy - 1 + c2
                    y_copy(p, g, g, whole, other).wait_recv()
                    if c2 == 0:
                        @pl.when(y == dy)
                        def _():
                            n_copy(p, g, g, other).wait_recv()
        @pl.when((y == 0) & (c == 1))
        def _():
            n_copy(p, 0, 0, other).wait_recv()

    cut = (slots + 1) // 2
    spans = (pl.ds(blocks, cut), pl.ds(blocks + cut, slots - cut))

    def compact(p):
        zero_group = jnp.where(y == 0, jnp.where(c == 0, 7, 0), 2 * y - 1)
        tiles[p][blocks, x] = rp[p][zero_group * SPAN + 8]
        for b in range(blocks):
            for j in range(picks):
                tiles[p][blocks + 1 + b * picks + j, x] = rp[p][slot_source(b, j)]

    def x_copy(p, span, of, sem, way):
        region = tiles[p].at[spans[span], of]
        return remote(region, region, xsend.at[p, sem], xrecv.at[p, sem], (x_right, x_left)[way])

    def x_start(p):
        x_copy(p, 0, x, 0, 0).start()
        x_copy(p, 1, x, 3, 1).start()
        x_copy(p, 1, x, 1, 0).start()
        x_copy(p, 0, x, 2, 1).start()

    def x_forward(p):
        x_copy(p, 0, xl, 0, 0).wait_recv()
        x_copy(p, 0, xl, 4, 0).start()
        x_copy(p, 1, xr, 3, 1).wait_recv()
        x_copy(p, 1, xr, 5, 1).start()

    def x_finish(p):
        x_copy(p, 1, xl, 1, 0).wait_recv()
        x_copy(p, 0, xr, 2, 1).wait_recv()
        x_copy(p, 0, xo, 4, 0).wait_recv()
        x_copy(p, 1, xo, 5, 1).wait_recv()

    def step(p, k):
        y_wait(p)
        compact(p)
        x_start(p)

    factor = math.log2(math.e) / math.sqrt(head)
    lanes = 128

    def score(q, keys):
        return lax.dot_general(q, keys, (((1,), (1,)), ((), ())), preferred_element_type=jnp.float32)

    def chunks(b):
        for h in range(heads):
            for r in range(2):
                start = pl.multiple_of(b * block_len, block_len) + r * half
                yield (b * heads + h) * 2 + r, r, pl.ds(start, half), pl.ds(h * head, head)

    def own_part(b0, b1):
        def body(b, _):
            for i, r, at_rows, at_head in chunks(b):
                own = (r + 1) * half
                t = score(q_vm[at_rows, at_head], k_vm[b].reshape(block_len, head)[:own])
                row = lax.broadcasted_iota(jnp.int32, (half, own), 0) + r * half
                col = lax.broadcasted_iota(jnp.int32, (half, own), 1)
                t = jnp.where(col <= row, t, -1e30)
                top = jnp.broadcast_to(jnp.max(t, axis=1, keepdims=True), (half, lanes))
                m_ref[i] = top
                shift = top * factor
                total = jnp.zeros((half, lanes), jnp.float32)
                out = jnp.zeros((half, head), jnp.float32)
                ps = []
                for n in range(own // lanes):
                    e = jnp.exp2(t[:, n * lanes:(n + 1) * lanes] * factor - shift)
                    total += e
                    ps.append(e.astype(jnp.bfloat16))
                l_ref[i] = total
                acc_ref[i] = jnp.dot(
                    jnp.concatenate(ps, axis=1),
                    v_vm[b].reshape(block_len, head)[:own],
                    preferred_element_type=jnp.float32,
                )
            return 0

        lax.fori_loop(b0, b1, body, 0)

    def soft_part(p, b0, b1, last):
        def body(b, _):
            picked = [tile_of(b, j) for j in range(picks + 1)]
            for i, r, at_rows, at_head in chunks(b):
                q = q_vm[at_rows, at_head]
                top = m_ref[i]
                old = top
                for j in range(picks + 1):
                    t = score(q, tiles[p][picked[j]].reshape(half, head))
                    sc[:, pl.ds(j * half, half)] = t
                    top = jnp.maximum(top, jnp.max(t, axis=1, keepdims=True))
                shift = top * factor
                scale = jnp.exp2(old * factor - shift)
                total = l_ref[i] * scale
                for j in range(picks + 1):
                    part = jnp.zeros((half, lanes), jnp.float32)
                    for n in range(j * half // lanes, (j + 1) * half // lanes):
                        e = jnp.exp2(sc[:, pl.ds(n * lanes, lanes)] * factor - shift)
                        part += e
                        prob[i, :, pl.ds(n * lanes, lanes)] = e.astype(jnp.bfloat16)
                    total += part * jnp.where(picked[j] == null, 0.0, 1.0)
                if last:
                    full = jnp.sum(total, axis=1, keepdims=True)
                    total = jnp.broadcast_to(1.0 / full, (half, lanes))
                l_ref[i] = total
                m_ref[i] = top
                acc_ref[i] = acc_ref[i] * scale
            return 0

        lax.fori_loop(b0, b1, body, 0)

    def out_copy(b):
        at_rows = pl.ds(pl.multiple_of(b * block_len, block_len), block_len)
        return pltpu.make_async_copy(out_vm.at[at_rows], out_hbm.at[at_rows], out_sem.at[b])

    def value_part(p, b0, b1, last):
        def body(b, _):
            picked = [tile_of(b, j) for j in range(picks + 1)]
            for i, r, at_rows, at_head in chunks(b):
                out = acc_ref[i]
                for j in range(picks + 1):
                    out += jnp.dot(
                        prob[i, :, pl.ds(j * half, half)],
                        tiles[p][picked[j]].reshape(half, head),
                        preferred_element_type=jnp.float32,
                    )
                if last:
                    out_vm[at_rows, at_head] = (out * l_ref[i]).astype(jnp.bfloat16)
                else:
                    acc_ref[i] = out
            if last:
                out_copy(b).start()
            return 0

        lax.fori_loop(b0, b1, body, 0)

    push(0, 0)
    z_start(1, 1)
    for copy in loads[PARTS:]:
        copy.wait()
    own_part(0, 2)
    z_wait(0, 1)
    z_start(0, 2)
    push(0, 1)
    push(1, 0)
    z_wait(0, 2)
    z_start(0, 3)
    push(0, 2)
    z_wait(1, 1)
    z_start(1, 2)
    own_part(2, 4)
    z_wait(0, 3)
    z_start(0, 4)
    push(0, 3)
    z_wait(1, 2)
    z_start(1, 3)
    z_wait(0, 4)
    push(0, 4)
    push(1, 1)
    push(1, 2)
    z_start(2, 1)
    z_wait(1, 3)
    z_start(1, 4)
    push(1, 3)
    push(2, 0)
    own_part(4, 6)
    z_wait(2, 1)
    z_start(2, 2)
    z_wait(1, 4)
    push(1, 4)
    z_start(3, 1)
    y_wait(0)
    compact(0)
    x_start(0)
    z_wait(2, 2)
    z_start(2, 3)
    push(2, 1)
    push(2, 2)
    z_wait(3, 1)
    z_start(3, 2)
    z_wait(2, 3)
    z_start(2, 4)
    push(2, 3)
    push(3, 0)
    x_forward(0)
    z_wait(3, 2)
    z_start(3, 3)
    z_wait(2, 4)
    push(2, 4)
    push(3, 1)
    push(3, 2)
    y_wait(1)
    compact(1)
    x_start(1)
    z_wait(3, 3)
    z_start(3, 4)
    push(3, 3)
    x_finish(0)
    first_key = jnp.broadcast_to(tiles[0][blocks, 0, :1, :].reshape(1, 1, head), (NX, rows, head))
    tiles[0][null] = first_key
    tiles[2][null] = first_key
    tiles[1][null] = jnp.zeros((NX, rows, head), jnp.bfloat16)
    tiles[3][null] = jnp.zeros((NX, rows, head), jnp.bfloat16)
    soft_part(0, 0, 2, False)
    z_wait(3, 4)
    push(3, 4)
    x_forward(1)
    soft_part(0, 2, 6, False)
    y_wait(2)
    compact(2)
    x_start(2)
    x_finish(1)
    value_part(1, 0, 3, False)
    x_forward(2)
    value_part(1, 3, 6, False)
    y_wait(3)
    compact(3)
    x_start(3)
    x_finish(2)
    soft_part(2, 0, 2, True)
    x_forward(3)
    soft_part(2, 2, 6, True)
    x_finish(3)
    value_part(3, 0, 6, True)

    for p in range(PARTS):
        for k in range(1, 5):
            for copy in z_copies(p, k):
                copy.wait_send()
        whole = (0, 8)
        y_copy(p, 0, 0, whole, other).wait_send()
        for dy in range(1, NY):
            @pl.when(y + dy < NY)
            def _():
                for c2 in range(NC):
                    g = 2 * dy - 1 + c2
                    y_copy(p, g, g, whole, other).wait_send()
        @pl.when((y == 0) & (c == 0))
        def _():
            for g in range(7):
                n_copy(p, 0, g, other).wait_send()
        x_copy(p, 0, x, 0, 0).wait_send()
        x_copy(p, 1, x, 3, 1).wait_send()
        x_copy(p, 1, x, 1, 0).wait_send()
        x_copy(p, 0, x, 2, 1).wait_send()
        x_copy(p, 0, xl, 4, 0).wait_send()
        x_copy(p, 1, xr, 5, 1).wait_send()
    table(0, 0, other).wait_send()
    for dy in range(1, NY):
        @pl.when(y >= dy)
        def _():
            for c2 in range(NC):
                table(0, 2 * dy - 1 + c2, other).wait_send()
    for b in range(blocks):
        out_copy(b).wait()


def shards(queries, keys, values, selected):
    blocks, picks = selected.shape
    head = keys.shape[1]
    block_len = keys.shape[0] // blocks
    heads = queries.shape[1] // head
    rows = block_len // (2 * NX)
    half = block_len // 2
    slots = blocks * picks + 1
    k5 = keys.reshape(blocks, NX, 2, rows, head)
    v5 = values.reshape(blocks, NX, 2, rows, head)
    part = lambda *shape: pltpu.VMEM(shape + (rows, head), jnp.bfloat16)
    wide = lambda *shape: pltpu.VMEM(shape, jnp.float32)
    hbm = pl.BlockSpec(memory_space=pl.ANY)
    dma = pltpu.SemaphoreType.DMA
    chunks = blocks * heads * 2
    return pl.pallas_call(
        functools.partial(fused, blocks, picks, block_len, heads),
        out_shape=jax.ShapeDtypeStruct(queries.shape, jnp.bfloat16),
        in_specs=[pl.BlockSpec(memory_space=pltpu.SMEM), hbm, hbm, hbm],
        out_specs=hbm,
        scratch_shapes=[part(blocks)] * 32
        + [part(7 * SPAN)] * 4
        + [part(GROUPS * SPAN)] * 4
        + [part()] * 4
        + [part(blocks + slots + 1, NX)] * 4
        + [
            pltpu.VMEM(queries.shape, jnp.bfloat16),
            part(blocks, NX, 2), part(blocks, NX, 2),
            pltpu.VMEM(queries.shape, jnp.bfloat16),
            pltpu.VMEM((chunks, half, (picks + 1) * half), jnp.bfloat16),
            wide(half, (picks + 1) * half),
            wide(chunks, half, 128), wide(chunks, half, 128), wide(chunks, half, head),
            pltpu.VMEM((8, 128), jnp.int32),
            pltpu.VMEM((7, 8, 128), jnp.int32), pltpu.SMEM((8, 8, 128), jnp.int32),
            dma((11,)), dma((8,)),
            dma((4, 4, 2)), dma((4, 4, 2)), dma((4, 7)), dma((4, 7)), dma((4, 7)), dma((4,)),
            dma((7,)), dma((7,)), dma((4, 6)), dma((4, 6)), dma((blocks,)),
        ],
        compiler_params=pltpu.CompilerParams(
            collective_id=0, has_side_effects=True, vmem_limit_bytes=56 * 2**20
        ),
    )(selected, queries, k5, v5)


def solution(mesh):
    in_specs = (P("seq", "head"), P("seq", None), P("seq", None), P("seq", None))
    return jax.shard_map(shards, mesh=mesh, in_specs=in_specs, out_specs=P("seq", "head"), check_vma=False)
```

time: 122 us -> 101 us (0.83); the launches traced: 120 us -> 101 us
  Pallas kernels: 114 us -> 97 us
  local copies, waits for them, and re-layouts: 5.65 us -> 4 us
    pallas_call x2 -> x1, Pallas kernels: 114 us -> 97 us  [shards(): pl.pallas_call(functools.partial(fused, blocks, picks, block_len, heads),...]
    unnamed x11 -> x2, local copies, waits for them, and re-layouts: 5.29 us -> 4 us
where the time goes in v3:
time: 101 us
  Pallas kernels  97 us (96%)
  local copies, waits for them, and re-layouts  4 us (4%)
    pallas_call x1, Pallas kernels, shards(): pl.pallas_call(functools.partial(fused, blocks, picks, block_len, heads),...  97 us
    unnamed x2, local copies, waits for them, and re-layouts  4 us

profile of v3, /device:TPU:24, one launch (start us, length us, event | category | flops | bytes accessed | tf_op | source)
XLA Modules:
  0.0 101.0 jit_solution(6528948281408010032)
XLA Ops:
  0.0 1.4 %copy.5.sel = s32[6,3]{1,0:T(8,128)} copy(s32[6,3]{0,1:T(4,128)} %param.7) | data formatting | bytes 144 | tf_op args[3]
  1.4 97.0 %shard_map.46 = bf16[3072,256]{1,0:T(8,128)(2,1)} custom-call(s32[6,3]{1,0:T(8,128)} %copy.5.sel, bf16[3072,256]{1,0:T(8,128)(2,1)} %q_hbm.1, bf16[6,4,2,64,128]{4,3,2,1,0:T(8,128)(2,1)} %bitcast.2, bf16[6,4,2,64,128]{4,3,2,1,0:T(8,128)(2,1)} %bitcast.3), custom_call_target="tpu_custom_call" | custom-call | tf_op jit(solution)/shard_map/pallas_call | solution.py:498
  98.4 2.7 %copy.7 = bf16[3072,256]{1,0:T(8,128)(2,1)} copy(bf16[3072,256]{1,0:T(8,128)(2,1)} %shard_map.46) | data formatting | bytes 3145728

commit v4 on v3

--- a/solution.py
+++ b/solution.py
@@ -12,25 +12,25 @@
 NY, NZ, NC, NX = 4, 8, 2, 4
 GROUPS = 8
 SPAN = 9
-ARRIVAL = ((0,), (7, 1), (6, 2), (5, 3), (4,))
-STARTS = (0, 1, 3, 5, 7)
-PARTS = 4
+ARRIVAL = ((0, 7, 1), (6, 2), (5, 3, 4))
+STARTS = (0, 3, 5)
+SETS = 2
+PARTS = 2 * SETS
 
 
 def fused(blocks, picks, block_len, heads, sel, q_hbm, k_hbm, v_hbm, out_hbm, *scratch):
-    rows = block_len // (2 * NX)
+    rows = block_len // (SETS * NX)
     half = block_len // 2
     head = k_hbm.shape[-1]
     slots = blocks * picks + 1
     null = blocks + slots
-    zs = [scratch[8 * p:8 * p + 8] for p in range(PARTS)]
-    sp = scratch[32:36]
-    rp = scratch[36:40]
-    zero = scratch[40:44]
-    tiles = scratch[44:48]
-    (q_vm, k_vm, v_vm, out_vm, prob, sc, m_ref, l_ref, acc_ref, want_ref,
+    scratch = list(scratch)
+    take = lambda n: [scratch.pop(0) for _ in range(n)]
+    zs = [take(NZ) for _ in range(PARTS)]
+    sp, rp, zero, tiles = take(PARTS), take(PARTS), take(PARTS), take(PARTS)
+    (q_vm, k_vm, v_vm, out_vm, prob, sc, m_ref, l_ref, acc_ref, scale_ref, want_ref,
      tabs, tabs_smem, load_sem, tab_local, zsend, zrecv, ysend, yrecv, nsend, nrecv,
-     tsend, trecv, xsend, xrecv, out_sem) = scratch[48:]
+     tsend, trecv, xsend, xrecv, out_sem) = scratch
     s = lax.axis_index("seq")
     x = lax.axis_index("head")
     c = lax.rem(s, NC)
@@ -61,11 +61,21 @@
                 source(p).at[:, :, p // 2], tiles[p].at[pl.ds(0, blocks)], load_sem.at[PARTS + p]
             )
         )
-    loads.append(pltpu.make_async_copy(k_hbm, k_vm, load_sem.at[8]))
-    loads.append(pltpu.make_async_copy(v_hbm, v_vm, load_sem.at[9]))
-    loads.append(pltpu.make_async_copy(q_hbm, q_vm, load_sem.at[10]))
+    loads.append(pltpu.make_async_copy(k_hbm, k_vm, load_sem.at[2 * PARTS]))
+    loads.append(pltpu.make_async_copy(v_hbm, v_vm, load_sem.at[2 * PARTS + 1]))
+    loads.append(pltpu.make_async_copy(q_hbm, q_vm, load_sem.at[2 * PARTS + 2]))
     for copy in loads:
         copy.start()
+
+    lane = lax.broadcasted_iota(jnp.int32, (8, 128), 1)
+    want = jnp.zeros((8, 128), jnp.int32)
+    for b in range(blocks):
+        for j in range(picks):
+            chosen = sel[j, b]
+            owner = jnp.where(chosen != 0, chosen // blocks, -1)
+            want = jnp.where(lane == owner, lax.rem(chosen, blocks), want)
+    want_ref[...] = jnp.where(lane == s, 0, want)
+    tabs[...] = jnp.where(lane == s, 0, want)
 
     barrier = pltpu.get_barrier_semaphore()
     partners = [right, left, other, x_right, x_left]
@@ -75,26 +85,15 @@
     for dev in partners:
         pl.semaphore_signal(barrier, inc=1, device_id=dev, device_id_type=MESH)
 
-    lane = lax.broadcasted_iota(jnp.int32, (8, 128), 1)
-    want = jnp.zeros((8, 128), jnp.int32)
-    for b in range(blocks):
-        for j in range(picks):
-            chosen = sel[b, j]
-            owner = jnp.where(chosen != 0, chosen // blocks, -1)
-            want = jnp.where(lane == owner, lax.rem(chosen, blocks), want)
-    want_ref[...] = jnp.where(lane == s, 0, want)
-    own_table = pltpu.make_async_copy(want_ref, tabs_smem.at[7], tab_local.at[7])
-    own_table.start()
-
     def live(b, j):
-        chosen = sel[b, j]
+        chosen = sel[j, b]
         ok = chosen != 0
         for i in range(j):
-            ok = ok & (chosen != sel[b, i])
+            ok = ok & (chosen != sel[i, b])
         return ok
 
     def slot_source(b, j):
-        owner = sel[b, j] // blocks
+        owner = sel[j, b] // blocks
         oy, oz, oc = owner // (NZ * NC), lax.rem(owner // NC, NZ), lax.rem(owner, NC)
         dy, dz = y - oy, lax.rem(oz - z + NZ, NZ)
         group = jnp.where(dy == 0, jnp.where(oc == c, 7, 0), 2 * dy - 1 + oc)
@@ -104,7 +103,7 @@
     def tile_of(b, j):
         if j == 0:
             return jnp.where(s * blocks + b != 0, blocks, null)
-        chosen = sel[b, j - 1]
+        chosen = sel[j - 1, b]
         here = jnp.where(chosen // blocks == s, lax.rem(chosen, blocks), blocks + 1 + b * picks + (j - 1))
         return jnp.where(live(b, j - 1), here, null)
 
@@ -133,10 +132,7 @@
     z_start(0, 1)
 
     def table(g_there, sem, dev):
-        return remote(want_ref, tabs.at[g_there], tsend.at[sem], trecv.at[g_there], dev)
-
-    def table_in(g):
-        return pltpu.make_async_copy(tabs.at[g], tabs_smem.at[g], tab_local.at[g])
+        return remote(want_ref.at[0], tabs.at[g_there], tsend.at[sem], trecv.at[g_there], dev)
 
     table(0, 0, other).start()
     for dy in range(1, NY):
@@ -144,22 +140,17 @@
         def _():
             for c2 in range(NC):
                 table(2 * dy - 1 + c, 2 * dy - 1 + c2, at(y - dy, z, c2)).start()
+    z_start(1, 1)
     table(0, 0, other).wait_recv()
-    table_in(0).start()
     for dy in range(1, NY):
         @pl.when(y + dy < NY)
         def _():
             for c2 in range(NC):
                 g = 2 * dy - 1 + c2
                 table(g, g, other).wait_recv()
-                table_in(g).start()
-    table_in(0).wait()
-    for dy in range(1, NY):
-        @pl.when(y + dy < NY)
-        def _():
-            for c2 in range(NC):
-                table_in(2 * dy - 1 + c2).wait()
-    own_table.wait()
+    tables_in = pltpu.make_async_copy(tabs, tabs_smem, tab_local.at[0])
+    tables_in.start()
+    tables_in.wait()
 
     def y_copy(p, g_here, g_there, place, dev):
         return remote(
@@ -176,7 +167,7 @@
 
         def pack(g):
             for j, d in enumerate(ARRIVAL[k]):
-                sp[p][g * SPAN + place[0] + j] = zs[p][d][tabs_smem[g, 0, owner_at(d)]]
+                sp[p][g * SPAN + place[0] + j] = zs[p][d][tabs_smem[g, owner_at(d)]]
 
         for dy in (2, 1, 3):
             @pl.when(y + dy < NY)
@@ -188,12 +179,12 @@
         pack(0)
         y_copy(p, 0, 0, place, other).start()
         for j, d in enumerate(ARRIVAL[k]):
-            rp[p][7 * SPAN + place[0] + j] = zs[p][d][tabs_smem[7, 0, owner_at(d)]]
+            rp[p][7 * SPAN + place[0] + j] = zs[p][d][tabs_smem[7, owner_at(d)]]
         for d in ARRIVAL[k]:
             @pl.when((y == 0) & (c == 0) & (z == (8 - d) % 8))
             def _():
                 zero[p][...] = zs[p][d][0]
-        if k == 4:
+        if k == len(ARRIVAL) - 1:
             push_zero(p)
 
     def n_copy(p, g_there, sem, dev):
@@ -257,11 +248,6 @@
         x_copy(p, 0, xr, 2, 1).wait_recv()
         x_copy(p, 0, xo, 4, 0).wait_recv()
         x_copy(p, 1, xo, 5, 1).wait_recv()
-
-    def step(p, k):
-        y_wait(p)
-        compact(p)
-        x_start(p)
 
     factor = math.log2(math.e) / math.sqrt(head)
     lanes = 128
@@ -303,33 +289,44 @@
 
         lax.fori_loop(b0, b1, body, 0)
 
-    def soft_part(p, b0, b1, last):
+    width = NX * rows
+    pair = half // width
+
+    def joined(p, picked, g):
+        return jnp.concatenate(
+            [tiles[p][picked[g * pair + n]].reshape(width, head) for n in range(pair)], axis=0
+        )
+
+    groups = (picks + 1) // pair
+
+    def soft_part(p, b0, b1):
+        last = p == PARTS - 2
+
         def body(b, _):
             picked = [tile_of(b, j) for j in range(picks + 1)]
+            weight = [jnp.where(tile == null, 0.0, 1.0) for tile in picked]
             for i, r, at_rows, at_head in chunks(b):
                 q = q_vm[at_rows, at_head]
-                top = m_ref[i]
-                old = top
-                for j in range(picks + 1):
-                    t = score(q, tiles[p][picked[j]].reshape(half, head))
-                    sc[:, pl.ds(j * half, half)] = t
+                old = m_ref[i]
+                top = old
+                for g in range(groups):
+                    t = score(q, joined(p, picked, g))
+                    sc[:, pl.ds(g * half, half)] = t
                     top = jnp.maximum(top, jnp.max(t, axis=1, keepdims=True))
                 shift = top * factor
                 scale = jnp.exp2(old * factor - shift)
                 total = l_ref[i] * scale
                 for j in range(picks + 1):
-                    part = jnp.zeros((half, lanes), jnp.float32)
-                    for n in range(j * half // lanes, (j + 1) * half // lanes):
+                    for n in range(j * width // lanes, (j + 1) * width // lanes):
                         e = jnp.exp2(sc[:, pl.ds(n * lanes, lanes)] * factor - shift)
-                        part += e
+                        total += e * weight[j]
                         prob[i, :, pl.ds(n * lanes, lanes)] = e.astype(jnp.bfloat16)
-                    total += part * jnp.where(picked[j] == null, 0.0, 1.0)
                 if last:
                     full = jnp.sum(total, axis=1, keepdims=True)
                     total = jnp.broadcast_to(1.0 / full, (half, lanes))
                 l_ref[i] = total
                 m_ref[i] = top
-                acc_ref[i] = acc_ref[i] * scale
+                scale_ref[i] = scale
             return 0
 
         lax.fori_loop(b0, b1, body, 0)
@@ -338,115 +335,116 @@
         at_rows = pl.ds(pl.multiple_of(b * block_len, block_len), block_len)
         return pltpu.make_async_copy(out_vm.at[at_rows], out_hbm.at[at_rows], out_sem.at[b])
 
-    def value_part(p, b0, b1, last):
+    def value_part(p, b0, b1):
+        last = p == PARTS - 1
+
         def body(b, _):
             picked = [tile_of(b, j) for j in range(picks + 1)]
-            for i, r, at_rows, at_head in chunks(b):
-                out = acc_ref[i]
-                for j in range(picks + 1):
+            for h in range(heads):
+                i = pl.ds((b * heads + h) * 2, 2)
+                out = (acc_ref[i] * scale_ref[i]).reshape(block_len, head)
+                for g in range(groups):
                     out += jnp.dot(
-                        prob[i, :, pl.ds(j * half, half)],
-                        tiles[p][picked[j]].reshape(half, head),
+                        prob[i, :, pl.ds(g * half, half)].reshape(block_len, half),
+                        joined(p, picked, g),
                         preferred_element_type=jnp.float32,
                     )
                 if last:
-                    out_vm[at_rows, at_head] = (out * l_ref[i]).astype(jnp.bfloat16)
+                    out = out * l_ref[i].reshape(block_len, lanes)
+                    at_rows = pl.ds(pl.multiple_of(b * block_len, block_len), block_len)
+                    out_vm[at_rows, pl.ds(h * head, head)] = out.astype(jnp.bfloat16)
                 else:
-                    acc_ref[i] = out
+                    acc_ref[i] = out.reshape(2, half, head)
             if last:
                 out_copy(b).start()
             return 0
 
         lax.fori_loop(b0, b1, body, 0)
 
-    push(0, 0)
-    z_start(1, 1)
+    def attend_part(p, b0, b1):
+        (soft_part, value_part)[p % 2](p, b0, b1)
+
+    def null_tiles():
+        first_key = jnp.broadcast_to(tiles[0][blocks, 0, :1, :].reshape(1, 1, head), (NX, rows, head))
+        for p in range(0, PARTS, 2):
+            tiles[p][null] = first_key
+            tiles[p + 1][null] = jnp.zeros((NX, rows, head), jnp.bfloat16)
+
+    def arrived(p):
+        y_wait(p)
+        compact(p)
+        x_start(p)
+
     for copy in loads[PARTS:]:
         copy.wait()
-    own_part(0, 2)
     z_wait(0, 1)
     z_start(0, 2)
-    push(0, 1)
+    push(0, 0)
+    z_wait(1, 1)
+    z_start(1, 2)
     push(1, 0)
+    own_part(0, 1)
     z_wait(0, 2)
     z_start(0, 3)
-    push(0, 2)
-    z_wait(1, 1)
-    z_start(1, 2)
-    own_part(2, 4)
+    push(0, 1)
+    z_wait(1, 2)
+    z_start(1, 3)
+    own_part(1, 2)
     z_wait(0, 3)
     z_start(0, 4)
-    push(0, 3)
-    z_wait(1, 2)
-    z_start(1, 3)
+    z_start(2, 1)
+    own_part(2, 3)
     z_wait(0, 4)
-    push(0, 4)
-    push(1, 1)
-    push(1, 2)
-    z_start(2, 1)
+    push(0, 2)
     z_wait(1, 3)
     z_start(1, 4)
-    push(1, 3)
-    push(2, 0)
-    own_part(4, 6)
+    push(1, 1)
     z_wait(2, 1)
     z_start(2, 2)
+    arrived(0)
     z_wait(1, 4)
-    push(1, 4)
+    push(1, 2)
     z_start(3, 1)
-    y_wait(0)
-    compact(0)
-    x_start(0)
+    own_part(3, 4)
     z_wait(2, 2)
     z_start(2, 3)
-    push(2, 1)
-    push(2, 2)
+    push(2, 0)
+    x_forward(0)
     z_wait(3, 1)
     z_start(3, 2)
+    push(2, 1)
+    arrived(1)
     z_wait(2, 3)
     z_start(2, 4)
-    push(2, 3)
-    push(3, 0)
-    x_forward(0)
+    own_part(4, 6)
+    z_wait(2, 4)
+    push(2, 2)
     z_wait(3, 2)
     z_start(3, 3)
-    z_wait(2, 4)
-    push(2, 4)
+    push(3, 0)
+    x_forward(1)
     push(3, 1)
-    push(3, 2)
-    y_wait(1)
-    compact(1)
-    x_start(1)
+    x_finish(0)
+    null_tiles()
+    attend_part(0, 0, 1)
     z_wait(3, 3)
     z_start(3, 4)
-    push(3, 3)
-    x_finish(0)
-    first_key = jnp.broadcast_to(tiles[0][blocks, 0, :1, :].reshape(1, 1, head), (NX, rows, head))
-    tiles[0][null] = first_key
-    tiles[2][null] = first_key
-    tiles[1][null] = jnp.zeros((NX, rows, head), jnp.bfloat16)
-    tiles[3][null] = jnp.zeros((NX, rows, head), jnp.bfloat16)
-    soft_part(0, 0, 2, False)
+    attend_part(0, 1, 2)
+    arrived(2)
     z_wait(3, 4)
-    push(3, 4)
-    x_forward(1)
-    soft_part(0, 2, 6, False)
-    y_wait(2)
-    compact(2)
-    x_start(2)
+    push(3, 2)
+    attend_part(0, 2, 4)
+    x_forward(2)
+    attend_part(0, 4, 6)
     x_finish(1)
-    value_part(1, 0, 3, False)
-    x_forward(2)
-    value_part(1, 3, 6, False)
-    y_wait(3)
-    compact(3)
-    x_start(3)
+    attend_part(1, 0, 6)
+    arrived(3)
     x_finish(2)
-    soft_part(2, 0, 2, True)
+    attend_part(2, 0, 2)
     x_forward(3)
-    soft_part(2, 2, 6, True)
+    attend_part(2, 2, 6)
     x_finish(3)
-    value_part(3, 0, 6, True)
+    attend_part(3, 0, 6)
 
     for p in range(PARTS):
         for k in range(1, 5):
@@ -485,11 +483,11 @@
     head = keys.shape[1]
     block_len = keys.shape[0] // blocks
     heads = queries.shape[1] // head
-    rows = block_len // (2 * NX)
+    rows = block_len // (SETS * NX)
     half = block_len // 2
     slots = blocks * picks + 1
-    k5 = keys.reshape(blocks, NX, 2, rows, head)
-    v5 = values.reshape(blocks, NX, 2, rows, head)
+    k5 = keys.reshape(blocks, NX, SETS, rows, head)
+    v5 = values.reshape(blocks, NX, SETS, rows, head)
     part = lambda *shape: pltpu.VMEM(shape + (rows, head), jnp.bfloat16)
     wide = lambda *shape: pltpu.VMEM(shape, jnp.float32)
     hbm = pl.BlockSpec(memory_space=pl.ANY)
@@ -500,28 +498,29 @@
         out_shape=jax.ShapeDtypeStruct(queries.shape, jnp.bfloat16),
         in_specs=[pl.BlockSpec(memory_space=pltpu.SMEM), hbm, hbm, hbm],
         out_specs=hbm,
-        scratch_shapes=[part(blocks)] * 32
-        + [part(7 * SPAN)] * 4
-        + [part(GROUPS * SPAN)] * 4
-        + [part()] * 4
-        + [part(blocks + slots + 1, NX)] * 4
+        scratch_shapes=[part(blocks)] * (PARTS * NZ)
+        + [part(7 * SPAN)] * PARTS
+        + [part(GROUPS * SPAN)] * PARTS
+        + [part()] * PARTS
+        + [part(blocks + slots + 1, NX)] * PARTS
         + [
             pltpu.VMEM(queries.shape, jnp.bfloat16),
-            part(blocks, NX, 2), part(blocks, NX, 2),
+            part(blocks, NX, SETS), part(blocks, NX, SETS),
             pltpu.VMEM(queries.shape, jnp.bfloat16),
-            pltpu.VMEM((chunks, half, (picks + 1) * half), jnp.bfloat16),
-            wide(half, (picks + 1) * half),
-            wide(chunks, half, 128), wide(chunks, half, 128), wide(chunks, half, head),
+            pltpu.VMEM((chunks, half, (picks + 1) * NX * rows), jnp.bfloat16),
+            wide(half, (picks + 1) * NX * rows),
+            wide(chunks, half, 128), wide(chunks, half, 128), wide(chunks, half, head), wide(chunks, half, 128),
             pltpu.VMEM((8, 128), jnp.int32),
-            pltpu.VMEM((7, 8, 128), jnp.int32), pltpu.SMEM((8, 8, 128), jnp.int32),
-            dma((11,)), dma((8,)),
-            dma((4, 4, 2)), dma((4, 4, 2)), dma((4, 7)), dma((4, 7)), dma((4, 7)), dma((4,)),
-            dma((7,)), dma((7,)), dma((4, 6)), dma((4, 6)), dma((blocks,)),
+            pltpu.VMEM((8, 128), jnp.int32), pltpu.SMEM((8, 128), jnp.int32),
+            dma((2 * PARTS + 3,)), dma((1,)),
+            dma((PARTS, 4, 2)), dma((PARTS, 4, 2)),
+            dma((PARTS, 7)), dma((PARTS, 7)), dma((PARTS, 7)), dma((PARTS,)),
+            dma((7,)), dma((7,)), dma((PARTS, 6)), dma((PARTS, 6)), dma((blocks,)),
         ],
         compiler_params=pltpu.CompilerParams(
             collective_id=0, has_side_effects=True, vmem_limit_bytes=56 * 2**20
         ),
-    )(selected, queries, k5, v5)
+    )(selected.T, queries, k5, v5)
 
 
 def solution(mesh):

time: 101 us -> 93.8 us (0.929)
  Pallas kernels: 97 us -> 91 us
  local copies, waits for them, and re-layouts: 4 us -> 2.65 us
    pallas_call x1, Pallas kernels: 97 us -> 91 us  [shards(): pl.pallas_call(functools.partial(fused, blocks, picks, block_len, heads),...]
    unnamed x2 -> x1, local copies, waits for them, and re-layouts: 4 us -> 2.65 us
where the time goes in v4:
time: 93.8 us; the launch traced here: 93.7 us
  Pallas kernels  91 us (97%)
  local copies, waits for them, and re-layouts  2.65 us (3%)
    pallas_call x1, Pallas kernels, shards(): pl.pallas_call(functools.partial(fused, blocks, picks, block_len, heads),...  91 us
    unnamed x1, local copies, waits for them, and re-layouts  2.65 us

profile of v4, /device:TPU:24, one launch (start us, length us, event | category | flops | bytes accessed | tf_op | source)
XLA Modules:
  0.0 93.7 jit_solution(7011685091255531203)
XLA Ops:
  0.0 91.0 %shard_map.46 = bf16[3072,256]{1,0:T(8,128)(2,1)} custom-call(s32[3,6]{1,0:T(4,128)} %bitcast.5, bf16[3072,256]{1,0:T(8,128)(2,1)} %q_hbm.1, bf16[6,4,2,64,128]{4,3,2,1,0:T(8,128)(2,1)} %bitcast.3, bf16[6,4,2,64,128]{4,3,2,1,0:T(8,128)(2,1)} %bitcast.4), custom_call_target="tpu_custom_call" | custom-call | tf_op jit(solution)/shard_map/pallas_call | solution.py:496
  91.0 2.7 %copy.6 = bf16[3072,256]{1,0:T(8,128)(2,1)} copy(bf16[3072,256]{1,0:T(8,128)(2,1)} %shard_map.46) | data formatting | bytes 3145728

commit v5 on v4

--- a/solution.py
+++ b/solution.py
@@ -15,7 +15,8 @@
 ARRIVAL = ((0, 7, 1), (6, 2), (5, 3, 4))
 STARTS = (0, 3, 5)
 SETS = 2
-PARTS = 2 * SETS
+TILES = 2 * SETS
+PARTS = ((0, 0, 64), (1, 0, 64), (2, 0, 64), (3, 0, 32), (3, 32, 32))
 
 
 def fused(blocks, picks, block_len, heads, sel, q_hbm, k_hbm, v_hbm, out_hbm, *scratch):
@@ -26,8 +27,9 @@
     null = blocks + slots
     scratch = list(scratch)
     take = lambda n: [scratch.pop(0) for _ in range(n)]
-    zs = [take(NZ) for _ in range(PARTS)]
-    sp, rp, zero, tiles = take(PARTS), take(PARTS), take(PARTS), take(PARTS)
+    count = len(PARTS)
+    zs = [take(NZ) for _ in range(count)]
+    sp, rp, zero, tiles = take(count), take(count), take(count), take(TILES)
     (q_vm, k_vm, v_vm, out_vm, prob, sc, m_ref, l_ref, acc_ref, scale_ref, want_ref,
      tabs, tabs_smem, load_sem, tab_local, zsend, zrecv, ysend, yrecv, nsend, nrecv,
      tsend, trecv, xsend, xrecv, out_sem) = scratch
@@ -51,19 +53,25 @@
             src_ref=src, dst_ref=dst, send_sem=ss, recv_sem=rs, device_id=dev, device_id_type=MESH
         )
 
-    def source(p):
-        return (k_hbm, v_hbm)[p % 2]
-
-    loads = [pltpu.make_async_copy(source(p).at[:, x, p // 2], zs[p][0], load_sem.at[p]) for p in range(PARTS)]
-    for p in range(PARTS):
+    def source(tile):
+        return (k_hbm, v_hbm)[tile % 2]
+
+    loads = []
+    for p, (tile, row, size) in enumerate(PARTS):
         loads.append(
             pltpu.make_async_copy(
-                source(p).at[:, :, p // 2], tiles[p].at[pl.ds(0, blocks)], load_sem.at[PARTS + p]
+                source(tile).at[:, x, tile // 2, pl.ds(row, size)], zs[p][0], load_sem.at[p]
             )
         )
-    loads.append(pltpu.make_async_copy(k_hbm, k_vm, load_sem.at[2 * PARTS]))
-    loads.append(pltpu.make_async_copy(v_hbm, v_vm, load_sem.at[2 * PARTS + 1]))
-    loads.append(pltpu.make_async_copy(q_hbm, q_vm, load_sem.at[2 * PARTS + 2]))
+    for tile in range(TILES):
+        loads.append(
+            pltpu.make_async_copy(
+                source(tile).at[:, :, tile // 2], tiles[tile].at[pl.ds(0, blocks)], load_sem.at[count + tile]
+            )
+        )
+    loads.append(pltpu.make_async_copy(k_hbm, k_vm, load_sem.at[count + TILES]))
+    loads.append(pltpu.make_async_copy(v_hbm, v_vm, load_sem.at[count + TILES + 1]))
+    loads.append(pltpu.make_async_copy(q_hbm, q_vm, load_sem.at[count + TILES + 2]))
     for copy in loads:
         copy.start()
 
@@ -107,7 +115,7 @@
         here = jnp.where(chosen // blocks == s, lax.rem(chosen, blocks), blocks + 1 + b * picks + (j - 1))
         return jnp.where(live(b, j - 1), here, null)
 
-    for copy in loads[:PARTS]:
+    for copy in loads[:count]:
         copy.wait()
     pl.semaphore_wait(barrier, len(partners))
 
@@ -222,13 +230,15 @@
 
     def compact(p):
         zero_group = jnp.where(y == 0, jnp.where(c == 0, 7, 0), 2 * y - 1)
-        tiles[p][blocks, x] = rp[p][zero_group * SPAN + 8]
+        tile, row, size = PARTS[p]
+        tiles[tile][blocks, x, row:row + size] = rp[p][zero_group * SPAN + 8]
         for b in range(blocks):
             for j in range(picks):
-                tiles[p][blocks + 1 + b * picks + j, x] = rp[p][slot_source(b, j)]
+                tiles[tile][blocks + 1 + b * picks + j, x, row:row + size] = rp[p][slot_source(b, j)]
 
     def x_copy(p, span, of, sem, way):
-        region = tiles[p].at[spans[span], of]
+        tile, row, size = PARTS[p]
+        region = tiles[tile].at[spans[span], of, pl.ds(row, size)]
         return remote(region, region, xsend.at[p, sem], xrecv.at[p, sem], (x_right, x_left)[way])
 
     def x_start(p):
@@ -300,7 +310,7 @@
     groups = (picks + 1) // pair
 
     def soft_part(p, b0, b1):
-        last = p == PARTS - 2
+        last = p == TILES - 2
 
         def body(b, _):
             picked = [tile_of(b, j) for j in range(picks + 1)]
@@ -336,7 +346,7 @@
         return pltpu.make_async_copy(out_vm.at[at_rows], out_hbm.at[at_rows], out_sem.at[b])
 
     def value_part(p, b0, b1):
-        last = p == PARTS - 1
+        last = p == TILES - 1
 
         def body(b, _):
             picked = [tile_of(b, j) for j in range(picks + 1)]
@@ -366,7 +376,7 @@
 
     def null_tiles():
         first_key = jnp.broadcast_to(tiles[0][blocks, 0, :1, :].reshape(1, 1, head), (NX, rows, head))
-        for p in range(0, PARTS, 2):
+        for p in range(0, TILES, 2):
             tiles[p][null] = first_key
             tiles[p + 1][null] = jnp.zeros((NX, rows, head), jnp.bfloat16)
 
@@ -375,7 +385,7 @@
         compact(p)
         x_start(p)
 
-    for copy in loads[PARTS:]:
+    for copy in loads[count:]:
         copy.wait()
     z_wait(0, 1)
     z_start(0, 2)
@@ -405,6 +415,7 @@
     z_wait(1, 4)
     push(1, 2)
     z_start(3, 1)
+    z_start(4, 1)
     own_part(3, 4)
     z_wait(2, 2)
     z_start(2, 3)
@@ -413,6 +424,8 @@
     z_wait(3, 1)
     z_start(3, 2)
     push(2, 1)
+    z_wait(4, 1)
+    z_start(4, 2)
     arrived(1)
     z_wait(2, 3)
     z_start(2, 4)
@@ -422,31 +435,45 @@
     z_wait(3, 2)
     z_start(3, 3)
     push(3, 0)
-    x_forward(1)
+    z_wait(4, 2)
+    z_start(4, 3)
     push(3, 1)
     x_finish(0)
     null_tiles()
     attend_part(0, 0, 1)
+    x_forward(1)
+    attend_part(0, 1, 2)
     z_wait(3, 3)
     z_start(3, 4)
-    attend_part(0, 1, 2)
+    z_wait(4, 3)
+    z_start(4, 4)
+    push(4, 0)
+    attend_part(0, 2, 3)
     arrived(2)
     z_wait(3, 4)
     push(3, 2)
-    attend_part(0, 2, 4)
+    z_wait(4, 4)
+    push(4, 1)
+    push(4, 2)
+    attend_part(0, 3, 5)
     x_forward(2)
-    attend_part(0, 4, 6)
+    attend_part(0, 5, 6)
     x_finish(1)
-    attend_part(1, 0, 6)
+    attend_part(1, 0, 2)
     arrived(3)
+    attend_part(1, 2, 6)
     x_finish(2)
-    attend_part(2, 0, 2)
+    attend_part(2, 0, 1)
+    arrived(4)
     x_forward(3)
-    attend_part(2, 2, 6)
+    attend_part(2, 1, 3)
+    x_forward(4)
+    attend_part(2, 3, 6)
     x_finish(3)
+    x_finish(4)
     attend_part(3, 0, 6)
 
-    for p in range(PARTS):
+    for p in range(count):
         for k in range(1, 5):
             for copy in z_copies(p, k):
                 copy.wait_send()
@@ -489,6 +516,8 @@
     k5 = keys.reshape(blocks, NX, SETS, rows, head)
     v5 = values.reshape(blocks, NX, SETS, rows, head)
     part = lambda *shape: pltpu.VMEM(shape + (rows, head), jnp.bfloat16)
+    sized = lambda *shape: [pltpu.VMEM(shape + (size, head), jnp.bfloat16) for _, _, size in PARTS]
+    count = len(PARTS)
     wide = lambda *shape: pltpu.VMEM(shape, jnp.float32)
     hbm = pl.BlockSpec(memory_space=pl.ANY)
     dma = pltpu.SemaphoreType.DMA
@@ -498,11 +527,11 @@
         out_shape=jax.ShapeDtypeStruct(queries.shape, jnp.bfloat16),
         in_specs=[pl.BlockSpec(memory_space=pltpu.SMEM), hbm, hbm, hbm],
         out_specs=hbm,
-        scratch_shapes=[part(blocks)] * (PARTS * NZ)
-        + [part(7 * SPAN)] * PARTS
-        + [part(GROUPS * SPAN)] * PARTS
-        + [part()] * PARTS
-        + [part(blocks + slots + 1, NX)] * PARTS
+        scratch_shapes=[ref for ref in sized(blocks) for _ in range(NZ)]
+        + sized(7 * SPAN)
+        + sized(GROUPS * SPAN)
+        + sized()
+        + [part(blocks + slots + 1, NX)] * TILES
         + [
             pltpu.VMEM(queries.shape, jnp.bfloat16),
             part(blocks, NX, SETS), part(blocks, NX, SETS),
@@ -512,10 +541,10 @@
             wide(chunks, half, 128), wide(chunks, half, 128), wide(chunks, half, head), wide(chunks, half, 128),
             pltpu.VMEM((8, 128), jnp.int32),
             pltpu.VMEM((8, 128), jnp.int32), pltpu.SMEM((8, 128), jnp.int32),
-            dma((2 * PARTS + 3,)), dma((1,)),
-            dma((PARTS, 4, 2)), dma((PARTS, 4, 2)),
-            dma((PARTS, 7)), dma((PARTS, 7)), dma((PARTS, 7)), dma((PARTS,)),
-            dma((7,)), dma((7,)), dma((PARTS, 6)), dma((PARTS, 6)), dma((blocks,)),
+            dma((count + TILES + 3,)), dma((1,)),
+            dma((count, 4, 2)), dma((count, 4, 2)),
+            dma((count, 7)), dma((count, 7)), dma((count, 7)), dma((count,)),
+            dma((7,)), dma((7,)), dma((count, 6)), dma((count, 6)), dma((blocks,)),
         ],
         compiler_params=pltpu.CompilerParams(
             collective_id=0, has_side_effects=True, vmem_limit_bytes=56 * 2**20

time: 93.8 us -> 91.2 us (0.972)
  Pallas kernels: 91 us -> 88 us
    pallas_call x1, Pallas kernels: 91 us -> 88 us  [shards(): pl.pallas_call(functools.partial(fused, blocks, picks, block_len, heads),...]
where the time goes in v5:
time: 91.2 us; the launch traced here: 90.7 us
  Pallas kernels  88 us (96%)
  local copies, waits for them, and re-layouts  2.65 us (3%)
    pallas_call x1, Pallas kernels, shards(): pl.pallas_call(functools.partial(fused, blocks, picks, block_len, heads),...  88 us
    unnamed x1, local copies, waits for them, and re-layouts  2.65 us

profile of v5, /device:TPU:24, one launch (start us, length us, event | category | flops | bytes accessed | tf_op | source)
XLA Modules:
  0.0 90.7 jit_solution(3499409547957033020)
XLA Ops:
  0.0 88.0 %shard_map.46 = bf16[3072,256]{1,0:T(8,128)(2,1)} custom-call(s32[3,6]{1,0:T(4,128)} %bitcast.5, bf16[3072,256]{1,0:T(8,128)(2,1)} %q_hbm.1, bf16[6,4,2,64,128]{4,3,2,1,0:T(8,128)(2,1)} %bitcast.3, bf16[6,4,2,64,128]{4,3,2,1,0:T(8,128)(2,1)} %bitcast.4), custom_call_target="tpu_custom_call" | custom-call | tf_op jit(solution)/shard_map/pallas_call | solution.py:525
  88.0 2.7 %copy.6 = bf16[3072,256]{1,0:T(8,128)(2,1)} copy(bf16[3072,256]{1,0:T(8,128)(2,1)} %shard_map.46) | data formatting | bytes 3145728

commit v6 on v5

--- a/solution.py
+++ b/solution.py
@@ -322,15 +322,19 @@
                 for g in range(groups):
                     t = score(q, joined(p, picked, g))
                     sc[:, pl.ds(g * half, half)] = t
-                    top = jnp.maximum(top, jnp.max(t, axis=1, keepdims=True))
+                    for n in range(half // lanes):
+                        top = jnp.maximum(top, t[:, n * lanes:(n + 1) * lanes])
+                top = jnp.broadcast_to(jnp.max(top, axis=1, keepdims=True), (half, lanes))
                 shift = top * factor
                 scale = jnp.exp2(old * factor - shift)
                 total = l_ref[i] * scale
                 for j in range(picks + 1):
+                    part = jnp.zeros((half, lanes), jnp.float32)
                     for n in range(j * width // lanes, (j + 1) * width // lanes):
                         e = jnp.exp2(sc[:, pl.ds(n * lanes, lanes)] * factor - shift)
-                        total += e * weight[j]
+                        part += e
                         prob[i, :, pl.ds(n * lanes, lanes)] = e.astype(jnp.bfloat16)
+                    total += part * weight[j]
                 if last:
                     full = jnp.sum(total, axis=1, keepdims=True)
                     total = jnp.broadcast_to(1.0 / full, (half, lanes))

time: 91.2 us -> 90.7 us (level)
  no operation moved by 1% of the time
where the time goes in v6:
time: 90.7 us; the launch traced here: 90.1 us
  Pallas kernels  87.4 us (96%)
  local copies, waits for them, and re-layouts  2.65 us (3%)
    pallas_call x1, Pallas kernels, shards(): pl.pallas_call(functools.partial(fused, blocks, picks, block_len, heads),...  87.4 us
    unnamed x1, local copies, waits for them, and re-layouts  2.65 us

profile of v6, /device:TPU:24, one launch (start us, length us, event | category | flops | bytes accessed | tf_op | source)
XLA Modules:
  0.0 90.1 jit_solution(1012771508568044759)
XLA Ops:
  0.0 87.4 %shard_map.46 = bf16[3072,256]{1,0:T(8,128)(2,1)} custom-call(s32[3,6]{1,0:T(4,128)} %bitcast.5, bf16[3072,256]{1,0:T(8,128)(2,1)} %q_hbm.1, bf16[6,4,2,64,128]{4,3,2,1,0:T(8,128)(2,1)} %bitcast.3, bf16[6,4,2,64,128]{4,3,2,1,0:T(8,128)(2,1)} %bitcast.4), custom_call_target="tpu_custom_call" | custom-call | tf_op jit(solution)/shard_map/pallas_call | solution.py:529
  87.4 2.7 %copy.6 = bf16[3072,256]{1,0:T(8,128)(2,1)} copy(bf16[3072,256]{1,0:T(8,128)(2,1)} %shard_map.46) | data formatting | bytes 3145728
